TPU v7x, 512 devices: a whole 4x4x16 slice. The times are simulated.
512 devices in a mesh: row: 32 (over x_lo, z), col: 16 (over y, x_hi, core).
Axes of the slice: x: 4 (x_hi: 2, x_lo: 2; x = x_hi * 2 + x_lo), y: 4, z: 16, core: 2. Of those that a mesh axis runs over, the one named last changes fastest.
Arguments:
- activations: bfloat16 [4096, 8192], P('row', 'col'), may hold values from -6 to 6
- w_value: bfloat16 [8192, 4096], P('row', 'col'), may hold values from -0.125 to 0.125
- query_input: bfloat16 [4096, 4096], P('row', 'col'), may hold values from -6 to 6
- key_input: bfloat16 [4096, 4096], P('row', 'col'), may hold values from -6 to 6
- log_decay: float32 [32, 4096], P('col', 'row'), may hold values from -0.7 to 0, as said below
- write_rate: float32 [32, 4096], P('col', 'row'), may hold values from 0.02 to 0.2
- norm_gain: float32 [128], replicated, may hold values from 0.1 to 1.9
- out_grad: bfloat16 [4096, 4096], P('row', 'col'), may hold values from -6 to 6
Outputs:
- layer_out: bfloat16 [4096, 4096], P('row', 'col')
- d_input: bfloat16 [4096, 8192], P('row', 'col')
- d_query: bfloat16 [4096, 4096], P('row', 'col')
- d_key: bfloat16 [4096, 4096], P('row', 'col')
- d_w_value: float32 [8192, 4096], P('row', 'col')
Inputs may be any that keep to these rules, and one draw needn't show every extreme that they name: log_decay is never positive.
All inputs are finite; a program needn't handle non-finite values.
Results may differ from a plain program's by a relative error of at most 0.025.
Values may be sent and summed in bfloat16 or wider, within the bound.
A program may use at most 64 MiB of HBM per device.

v0:
```python
import jax
import jax.numpy as jnp
from jax import lax
from jax.sharding import PartitionSpec as P

exact_mode = lax.Precision.HIGHEST


def passed_along(value, axis, steps):
    count = lax.axis_size(axis)
    leading, last = (max(0, -steps), min(count, count - steps))
    return lax.ppermute(value, axis, [(source, source + steps) for source in range(leading, last)])


def head_norm(values, norm_gain):
    mean_sq = jnp.mean(values * values, axis=-1, keepdims=True)
    return values * lax.rsqrt(mean_sq + 1e-06) * norm_gain


def to_heads(matrix, heads_dev):
    return matrix.astype(jnp.float32).reshape(matrix.shape[0], heads_dev, -1).transpose(1, 0, 2)


def from_heads(tensor):
    return tensor.transpose(1, 0, 2).reshape(tensor.shape[1], -1)


def block_terms(values, queries, key_rows, log_decay, write_rate):
    length = values.shape[1]
    head_size = values.shape[2]
    unit_keys = key_rows * lax.rsqrt(jnp.sum(key_rows * key_rows, axis=-1, keepdims=True) + 1e-06)
    lower_tri = jnp.tril(jnp.ones((length, length), jnp.float32))
    identity = jnp.eye(length, dtype=jnp.float32)
    log_cumul = jnp.einsum("ts,hs->ht", lower_tri, log_decay, precision=exact_mode)
    log_gaps = log_cumul[:, :, None] - log_cumul[:, None, :]
    within = jnp.where(lower_tri > 0, jnp.exp(jnp.where(lower_tri > 0, log_gaps, 0.0)), 0.0)
    key_gram = jnp.einsum("htd,hsd->hts", unit_keys, unit_keys, precision=exact_mode)
    coupling = write_rate[:, :, None] * (within - identity) * key_gram
    system = identity + coupling
    decays = jnp.exp(log_cumul)
    targets = jnp.concatenate(
        [write_rate[:, :, None] * values, (write_rate * decays)[:, :, None] * unit_keys], axis=2
    )
    solved = jax.scipy.linalg.solve_triangular(system, targets, lower=True)
    fresh_rows = solved[:, :, :head_size]
    carry_rows = solved[:, :, head_size:]
    query_key = jnp.einsum("htd,hsd->hts", queries, unit_keys, precision=exact_mode) * within
    out_zero = jnp.einsum("hts,hsv->htv", query_key, fresh_rows, precision=exact_mode)
    query_eff = decays[:, :, None] * queries - jnp.einsum(
        "hts,hsk->htk", query_key, carry_rows, precision=exact_mode
    )
    log_total = log_cumul[:, -1:]
    tail_decay = jnp.exp(log_total - log_cumul)
    transition = jnp.exp(log_total)[:, :, None] * jnp.eye(
        head_size, dtype=jnp.float32
    ) - jnp.einsum("hsk,hs,hsl->hkl", carry_rows, tail_decay, unit_keys, precision=exact_mode)
    state_add = jnp.einsum(
        "hsv,hs,hsk->hvk", fresh_rows, tail_decay, unit_keys, precision=exact_mode
    )
    return (out_zero, query_eff, transition, state_add)


def shards(
    activations, w_value, query_input, key_input, log_decay, write_rate, norm_gain, out_grad
):
    tok_rows, head_cols = query_input.shape
    heads_dev = log_decay.shape[0]
    gathered = lax.all_gather(activations, "col", axis=1, tiled=True)
    weight_cols = lax.all_gather(w_value, "row", axis=0, tiled=True)
    value_sum = jnp.dot(gathered, weight_cols, preferred_element_type=jnp.float32)
    value_proj = value_sum.astype(jnp.bfloat16)
    chain_len = lax.axis_size("row")
    first_token = lax.axis_index("row") * tok_rows
    carry_on = jnp.where(first_token % (tok_rows * chain_len) == 0, 0.0, 1.0).astype(jnp.float32)

    def local_terms(values, queries, key_rows):
        return block_terms(values, queries, key_rows, log_decay, write_rate)

    (out_zero, query_eff, transition, state_add), pull_terms = jax.vjp(
        local_terms,
        to_heads(value_proj, heads_dev),
        to_heads(query_input, heads_dev),
        to_heads(key_input, heads_dev),
    )
    blank = jnp.zeros_like(transition)

    def relay_state(repeat, state_now):
        state_out = (
            jnp.einsum("hvk,hkl->hvl", state_now, transition, precision=exact_mode) + state_add
        )
        return carry_on * passed_along(state_out.astype(jnp.bfloat16), "row", 1).astype(
            state_out.dtype
        )

    state_in = lax.fori_loop(0, chain_len - 1, relay_state, blank)
    out_raw = out_zero + jnp.einsum("htk,hvk->htv", query_eff, state_in, precision=exact_mode)

    def normalize(values):
        return head_norm(values, norm_gain)

    normed, pull_norm = jax.vjp(normalize, out_raw)
    layer_out = from_heads(normed).astype(jnp.bfloat16)
    (d_raw,) = pull_norm(to_heads(out_grad, heads_dev))
    local_grad = jnp.einsum("htv,htk->hvk", d_raw, query_eff, precision=exact_mode)
    flipped = jnp.swapaxes(transition, 1, 2)

    def relay_grad(repeat, grad_now):
        grad_in = jnp.einsum("hvk,hkl->hvl", grad_now, flipped, precision=exact_mode) + local_grad
        return passed_along((carry_on * grad_in).astype(jnp.bfloat16), "row", -1).astype(
            jnp.float32
        )

    grad_out = lax.fori_loop(0, chain_len - 1, relay_grad, blank)
    d_query_eff = jnp.einsum("htv,hvk->htk", d_raw, state_in, precision=exact_mode)
    d_transition = jnp.einsum("hvk,hvl->hkl", state_in, grad_out, precision=exact_mode)
    value_grad, query_grad, key_grad = pull_terms((d_raw, d_query_eff, d_transition, grad_out))
    d_value = from_heads(value_grad).astype(jnp.bfloat16)
    d_query = from_heads(query_grad).astype(jnp.bfloat16)
    d_key = from_heads(key_grad).astype(jnp.bfloat16)
    partials = lax.dot_general(
        d_value, weight_cols, (((1,), (1,)), ((), ())), preferred_element_type=jnp.float32
    )
    d_input = lax.psum_scatter(
        partials.astype(jnp.bfloat16), "col", scatter_dimension=1, tiled=True
    )
    weight_term = lax.dot_general(
        gathered, d_value, (((0,), (0,)), ((), ())), preferred_element_type=jnp.float32
    ).astype(jnp.bfloat16)
    owned_rows = w_value.shape[0]
    stacked = weight_term.reshape(chain_len, owned_rows, weight_term.shape[1])
    received = lax.all_to_all(stacked, "row", split_axis=0, concat_axis=0, tiled=True)
    d_w_value = jnp.sum(received.astype(jnp.float32), axis=0)
    return (layer_out, d_input, d_query, d_key, d_w_value)


def solution(mesh):
    in_specs = (
        P("row", "col"),
        P("row", "col"),
        P("row", "col"),
        P("row", "col"),
        P("col", "row"),
        P("col", "row"),
        P(),
        P("row", "col"),
    )
    out_specs = (
        P("row", "col"),
        P("row", "col"),
        P("row", "col"),
        P("row", "col"),
        P("row", "col"),
    )
    return jax.shard_map(shards, mesh=mesh, in_specs=in_specs, out_specs=out_specs, check_vma=False)
```

profile of v0, /device:TPU:6, one launch (start us, length us, event | category | flops | bytes accessed | tf_op | source)
XLA Modules:
  0.0 925.0 jit_solution(4341749900111391875)
XLA Ops:
  14.9 19.7 %custom-call.10 = f32[2,1,128,128]{2,3,1,0:T(8,128)S(1)} custom-call(f32[2,1,128,128]{3,2,1,0:T(8,128)S(1)} %fusion.22), custom_call_target="InvertDiagBlocksLowerTriangular" | custom-call | tf_op jit(solution)/shard_map/jvp(jit(_solve_triangular))/vmap()/triangular_solve | solution.py:44
  35.1 41.7 %all-gather.3.cloned.1.call-done = bf16[128,8192]{1,0:T(8,128)(2,1)} async-done(((bf16[128,512]{1,0:T(8,128)(2,1)}), bf16[128,8192]{1,0:T(8,128)(2,1)}) %all-gather.3.cloned.1.call-update) | async-done | bytes 2097168 | tf_op jit(solution)/shard_map/all_gather | solution.py:68
  76.8 139.5 %all-gather.5.cloned.1.call-done = bf16[8192,256]{1,0:T(8,128)(2,1)} async-done(((bf16[256,256]{1,0:T(8,128)(2,1)}), bf16[8192,256]{1,0:T(8,128)(2,1)}) %all-gather.5.cloned.1.call-update) | async-done | bytes 4194320 | tf_op jit(solution)/shard_map/all_gather | solution.py:69
  223.2 267.3 %while.22 = (s32[]{:T(128)}, f32[2,128,128]{2,1,0:T(8,128)S(1)}, f32[]{:T(128)}, f32[2,128,128]{2,1,0:T(8,128)S(1)}, f32[2,128,128]{2,1,0:T(8,128)S(1)}, /*index=5*/s32[]{:T(128)}, s32[]{:T(128)}) while((s32[]{:T(128)}, f32[2,128,128]{2,1,0:T(8,128)S(1)}, f32[]{:T(128)}, f32[2,128,128]{2,1,0:T(8,128)S(1)}, ...), condition=%wide.region_2.3_spmd.clone, body=%wide.region_1.2_spmd.clone.sunk | while | flops 50495488 | bytes 917635 | solution.py:95
  251.2 6.4 collective-permute-done
  259.8 6.5 collective-permute-done
  311.5 6.8 collective-permute-done
  372.0 6.7 collective-permute-done
  423.9 6.6 collective-permute-done
  494.1 302.6 %while.23 = (s32[]{:T(128)}, f32[2,128,128]{2,1,0:T(8,128)S(1)}, f32[]{:T(128)}, f32[2,128,128]{2,1,0:T(8,128)S(1)}, f32[2,128,128]{2,1,0:T(8,128)S(1)}, /*index=5*/s32[]{:T(128)}, s32[]{:T(128)}) while((s32[]{:T(128)}, f32[2,128,128]{2,1,0:T(8,128)S(1)}, f32[]{:T(128)}, f32[2,128,128]{2,1,0:T(8,128)S(1)}, ...), condition=%wide.region_6.7_spmd.clone, body=%wide.region_5.6_spmd.clone.sunk | while | flops 50495488 | bytes 917635 | solution.py:113
  541.4 6.5 collective-permute-start.1
  550.1 6.5 collective-permute-start.1
  602.1 6.5 collective-permute-start.1
  662.5 6.5 collective-permute-start.1
  690.8 6.6 collective-permute-start.1
  697.4 6.8 collective-permute-done.1
  707.4 8.0 collective-permute-done.1
  720.5 14.4 %collective-permute-done.1 = bf16[2,128,128]{2,1,0:T(8,128)(2,1)S(1)} collective-permute-done((bf16[2,128,128]{2,1,0:T(8,128)(2,1)S(1)}, bf16[2,128,128]{2,1,0:T(8,128)(2,1)S(1)}, u32[]{:S(2)}, u32[]{:S(2)}) %collective-permute-start.1) | collective-permute-done | bytes 65568 | tf_op jit(solution)/shard_map/while/body/eval_jaxpr/ppermute | solution.py:12
  735.2 6.8 collective-permute-start.1
  757.2 10.5 %collective-permute-start.1 = (bf16[2,128,128]{2,1,0:T(8,128)(2,1)S(1)}, bf16[2,128,128]{2,1,0:T(8,128)(2,1)S(1)}, u32[]{:S(2)}, u32[]{:S(2)}) collective-permute-start(bf16[2,128,128]{2,1,0:T(8,128)(2,1)S(1)} %fusion.133), channel_id=1, source_target_pairs={{16,0},{32,16},{48,32},{64,48},{80,64},{96,80},{112,96},{128,112},... | collective-permute-start | bytes 196616 | tf_op jit(solution)/shard_map/while/body/eval_jaxpr/ppermute | solution.py:12
  767.7 9.2 collective-permute-done.1
  777.2 9.0 collective-permute-start.1
  807.7 6.7 all-to-all-start
  826.1 83.1 %all-to-all-done = bf16[32,256,256]{1,2,0:T(8,128)(2,1)} async-done(((bf16[32,256,256]{1,2,0:T(8,128)(2,1)}), bf16[32,256,256]{1,2,0:T(8,128)(2,1)}, u32[]{:S(2)}, u32[]{:S(2)}) %all-to-all-start) | async-done | bytes 4194336 | tf_op jit(solution)/shard_map/all_to_all | solution.py:131
  (352 shorter events, 487.2 us)
Async XLA Ops:
  7.2 69.6 %all-gather.3.cloned.1.call-start = ((), (), s32[]{:S(2)}) async-start(), calls=%async_computation.2 | async-start | bytes 2228224 | tf_op jit(solution)/shard_map/all_gather | solution.py:68
  7.9 208.4 %all-gather.5.cloned.1.call-start = ((), (), s32[]{:S(2)}) async-start(), calls=%async_computation.3 | async-start | bytes 4325376 | tf_op jit(solution)/shard_map/all_gather | solution.py:69
  249.2 8.4 collective-permute-start
  257.9 8.4 collective-permute-start
  309.6 8.7 collective-permute-start
  370.0 8.7 collective-permute-start
  421.9 8.5 collective-permute-start
  541.4 8.4 collective-permute-start.1
  550.1 8.4 collective-permute-start.1
  567.4 8.3 collective-permute-start.1
  593.2 8.6 collective-permute-start.1
  602.1 8.4 collective-permute-start.1
  653.7 8.5 collective-permute-start.1
  662.5 8.4 collective-permute-start.1
  679.8 10.7 %collective-permute-start.1 = (bf16[2,128,128]{2,1,0:T(8,128)(2,1)S(1)}, bf16[2,128,128]{2,1,0:T(8,128)(2,1)S(1)}, u32[]{:S(2)}, u32[]{:S(2)}) collective-permute-start(bf16[2,128,128]{2,1,0:T(8,128)(2,1)S(1)} %fusion.133), channel_id=1, source_target_pairs={{16,0},{32,16},{48,32},{64,48},{80,64},{96,80},{112,96},{128,112},... | collective-permute-start | bytes 196616 | tf_op jit(solution)/shard_map/while/body/eval_jaxpr/ppermute | solution.py:12
  690.8 13.4 %collective-permute-start.1 = (bf16[2,128,128]{2,1,0:T(8,128)(2,1)S(1)}, bf16[2,128,128]{2,1,0:T(8,128)(2,1)S(1)}, u32[]{:S(2)}, u32[]{:S(2)}) collective-permute-start(bf16[2,128,128]{2,1,0:T(8,128)(2,1)S(1)} %fusion.133), channel_id=1, source_target_pairs={{16,0},{32,16},{48,32},{64,48},{80,64},{96,80},{112,96},{128,112},... | collective-permute-start | bytes 196616 | tf_op jit(solution)/shard_map/while/body/eval_jaxpr/ppermute | solution.py:12
  704.5 10.9 %collective-permute-start.1 = (bf16[2,128,128]{2,1,0:T(8,128)(2,1)S(1)}, bf16[2,128,128]{2,1,0:T(8,128)(2,1)S(1)}, u32[]{:S(2)}, u32[]{:S(2)}) collective-permute-start(bf16[2,128,128]{2,1,0:T(8,128)(2,1)S(1)} %fusion.133), channel_id=1, source_target_pairs={{16,0},{32,16},{48,32},{64,48},{80,64},{96,80},{112,96},{128,112},... | collective-permute-start | bytes 196616 | tf_op jit(solution)/shard_map/while/body/eval_jaxpr/ppermute | solution.py:12
  715.7 19.2 %collective-permute-start.1 = (bf16[2,128,128]{2,1,0:T(8,128)(2,1)S(1)}, bf16[2,128,128]{2,1,0:T(8,128)(2,1)S(1)}, u32[]{:S(2)}, u32[]{:S(2)}) collective-permute-start(bf16[2,128,128]{2,1,0:T(8,128)(2,1)S(1)} %fusion.133), channel_id=1, source_target_pairs={{16,0},{32,16},{48,32},{64,48},{80,64},{96,80},{112,96},{128,112},... | collective-permute-start | bytes 196616 | tf_op jit(solution)/shard_map/while/body/eval_jaxpr/ppermute | solution.py:12
  735.2 11.5 %collective-permute-start.1 = (bf16[2,128,128]{2,1,0:T(8,128)(2,1)S(1)}, bf16[2,128,128]{2,1,0:T(8,128)(2,1)S(1)}, u32[]{:S(2)}, u32[]{:S(2)}) collective-permute-start(bf16[2,128,128]{2,1,0:T(8,128)(2,1)S(1)} %fusion.133), channel_id=1, source_target_pairs={{16,0},{32,16},{48,32},{64,48},{80,64},{96,80},{112,96},{128,112},... | collective-permute-start | bytes 196616 | tf_op jit(solution)/shard_map/while/body/eval_jaxpr/ppermute | solution.py:12
  747.0 9.9 %collective-permute-start.1 = (bf16[2,128,128]{2,1,0:T(8,128)(2,1)S(1)}, bf16[2,128,128]{2,1,0:T(8,128)(2,1)S(1)}, u32[]{:S(2)}, u32[]{:S(2)}) collective-permute-start(bf16[2,128,128]{2,1,0:T(8,128)(2,1)S(1)} %fusion.133), channel_id=1, source_target_pairs={{16,0},{32,16},{48,32},{64,48},{80,64},{96,80},{112,96},{128,112},... | collective-permute-start | bytes 196616 | tf_op jit(solution)/shard_map/while/body/eval_jaxpr/ppermute | solution.py:12
  757.2 19.7 %collective-permute-start.1 = (bf16[2,128,128]{2,1,0:T(8,128)(2,1)S(1)}, bf16[2,128,128]{2,1,0:T(8,128)(2,1)S(1)}, u32[]{:S(2)}, u32[]{:S(2)}) collective-permute-start(bf16[2,128,128]{2,1,0:T(8,128)(2,1)S(1)} %fusion.133), channel_id=1, source_target_pairs={{16,0},{32,16},{48,32},{64,48},{80,64},{96,80},{112,96},{128,112},... | collective-permute-start | bytes 196616 | tf_op jit(solution)/shard_map/while/body/eval_jaxpr/ppermute | solution.py:12
  777.2 10.9 %collective-permute-start.1 = (bf16[2,128,128]{2,1,0:T(8,128)(2,1)S(1)}, bf16[2,128,128]{2,1,0:T(8,128)(2,1)S(1)}, u32[]{:S(2)}, u32[]{:S(2)}) collective-permute-start(bf16[2,128,128]{2,1,0:T(8,128)(2,1)S(1)} %fusion.133), channel_id=1, source_target_pairs={{16,0},{32,16},{48,32},{64,48},{80,64},{96,80},{112,96},{128,112},... | collective-permute-start | bytes 196616 | tf_op jit(solution)/shard_map/while/body/eval_jaxpr/ppermute | solution.py:12
  807.7 101.6 %all-to-all-start = ((bf16[32,256,256]{1,2,0:T(8,128)(2,1)}), bf16[32,256,256]{1,2,0:T(8,128)(2,1)}, u32[]{:S(2)}, u32[]{:S(2)}) async-start(bf16[32,256,256]{1,2,0:T(8,128)(2,1)} %bitcast.142), calls=%async_computation.1 | async-start | bytes 8388608 | tf_op jit(solution)/shard_map/all_to_all | solution.py:131
  814.5 104.0 %reduce-scatter.2.cloned.1.call-start = ((), (), s32[]{:S(2)}) async-start(), calls=%async_computation.4 | async-start | bytes 2228224 | tf_op jit(solution)/shard_map/reduce_scatter | solution.py:123
  (68 other events, 2194.7 us)
Sparse Core Ops, SparseCore 0:
  11.2 65.5 all-gather.2
  78.9 137.4 all-gather.4
  820.6 97.7 reduce-scatter.1
where the time goes:
time: 929 us; the launch traced here: 925 us
  waiting for transfers between devices  569 us (61%)
  starting transfers between devices  260 us (28%)
  matrix products  41.6 us (4%)
  other arithmetic  27.4 us (3%)
  between operations  14.5 us (2%)
  local copies, waits for them, and re-layouts  10.9 us (1%)
    ppermute x62, waiting for transfers between devices, passed_along(): lax.ppermute(value, axis, [(source, source + steps) for source in range(l...  297 us
    ppermute x62, starting transfers between devices, passed_along(): lax.ppermute(value, axis, [(source, source + steps) for source in range(l...  253 us
    all_gather x1, waiting for transfers between devices, shards(): weight_cols = lax.all_gather(w_value, 'row', axis=0, tiled=True)  140 us
    all_to_all x1, waiting for transfers between devices, shards(): lax.all_to_all(stacked, 'row', split_axis=0, concat_axis=0, tiled=True)  83.1 us
    all_gather x1, waiting for transfers between devices, shards(): gathered = lax.all_gather(activations, 'col', axis=1, tiled=True)  41.7 us
    another operation x1, other arithmetic, block_terms(): solved = jax.scipy.linalg.solve_triangular(system, targets, lower=True)  19.7 us
  transfers between devices with their start and end apart: 66, of which 66 were waited for; matrix products, arithmetic and copies ran while one was open for 4% of the time, Pallas kernels for 0%

commit v1 on v0

v1 whole, which is shorter than its diff:
```python
import functools

import jax
import jax.numpy as jnp
from jax import lax
from jax.experimental import pallas as pl
from jax.experimental.pallas import tpu as pltpu
from jax.sharding import PartitionSpec as P

MESH = pl.DeviceIdType.MESH
f32 = jnp.float32
bf16 = jnp.bfloat16
NN = (((1,), (0,)), ((), ()))
NT = (((1,), (1,)), ((), ()))
TN = (((0,), (0,)), ((), ()))


def dot(a, b, dims):
    return lax.dot_general(a, b, dims, preferred_element_type=f32)


def halves(a):
    high = a.astype(bf16)
    return high, (a - high.astype(f32)).astype(bf16)


def dot_left(a, b, dims):
    high, low = halves(a)
    return dot(high, b, dims) + dot(low, b, dims)


def dot_both(a, b, dims):
    a_high, a_low = halves(a)
    b_high, b_low = halves(b)
    return dot(a_high, b_high, dims) + (dot(a_high, b_low, dims) + dot(a_low, b_high, dims))


def key_terms(h, q, x, ld, wr, st):
    n = x.shape[0]
    rows = lax.broadcasted_iota(jnp.int32, (n, n), 0)
    cols = lax.broadcasted_iota(jnp.int32, (n, n), 1)
    lower = rows >= cols
    strict = rows > cols
    eye = rows == cols

    def col_of(row):
        return jnp.sum(jnp.where(eye, row, 0.0), axis=1, keepdims=True)

    def row_of(col):
        return jnp.sum(jnp.where(eye, col, 0.0), axis=0, keepdims=True)

    xf = x.astype(f32)
    rs = lax.rsqrt(jnp.sum(xf * xf, axis=1, keepdims=True) + 1e-06)
    rs_row = row_of(rs)
    g = jnp.sum(jnp.where(lower, ld, 0.0), axis=1, keepdims=True)
    g_row = row_of(g)
    total = jnp.sum(ld, axis=1, keepdims=True)
    decay = jnp.exp(g)
    decay_row = jnp.exp(g_row)
    tail = jnp.exp(total - g)
    b = col_of(wr)
    within = jnp.where(lower, jnp.exp(jnp.where(lower, g - g_row, 0.0)), 0.0)
    gram = dot(x, x, NT) * (rs * rs_row)
    coupling = jnp.where(strict, b * within * gram, 0.0)
    ident = jnp.where(eye, 1.0, 0.0)
    near = jnp.where((rows // 16) == (cols // 16), coupling, 0.0)
    inv = ident - near
    power = near
    for _ in range(3):
        power = dot_both(power, power, NN)
        inv = inv + dot_both(inv, power, NN)
    size = 16
    while size < n:
        off = ((rows // (2 * size)) == (cols // (2 * size))) & ((rows // size) != (cols // size))
        part = jnp.where(off, coupling, 0.0)
        inv = inv - dot_both(dot_both(inv, part, NN), inv, NN)
        size *= 2
    carry = dot_left(inv * (wr * decay_row * rs_row), x, NN)
    read = dot(q, x, NT) * within * rs_row
    loss = dot_left(carry * (tail * rs), x, TN) + jnp.where(eye, 1.0 - jnp.exp(total), 0.0)
    st["inv"][h] = inv
    st["within"][h] = within
    st["carry"][h] = carry
    st["read"][h] = read
    lanes = jnp.zeros((n, 128), f32)
    lane = lax.broadcasted_iota(jnp.int32, (n, 128), 1)
    for i, c in enumerate((rs, decay, tail, b)):
        lanes = jnp.where(lane == i, c, lanes)
    st["cols"][h] = lanes
    st["loss"][h] = loss.astype(bf16)


def chain_kernel(
    v_ref, q_ref, x_ref, og_ref, ld_ref, wr_ref, gain_ref,
    out_ref, dq_ref, dk_ref, dv_ref,
    inv, within, carry, read, cols, loss, fresh, grad_raw, summed,
    add, add2, loss_all, got, got2, sent, sent2, state, grad,
    loss_send, loss_recv, s_send, s_recv, b_send, b_recv, t_send, t_recv, u_send, u_recv,
):
    n_row = 32
    me, col = lax.axis_index("row"), lax.axis_index("col")
    head = me // 16
    slot = (me % 16) // 2
    worker = me % 2 == 0
    st = dict(inv=inv, within=within, carry=carry, read=read, cols=cols, loss=loss)

    barrier = pltpu.get_barrier_semaphore()

    def greet(i, _):
        @pl.when(i != me)
        def _():
            pl.semaphore_signal(barrier, inc=1, device_id=(i, col), device_id_type=MESH)
        return 0

    lax.fori_loop(0, n_row, greet, 0)

    for h in range(2):
        part = slice(h * 128, (h + 1) * 128)
        key_terms(h, q_ref[:, part], x_ref[:, part], ld_ref[h : h + 1, :], wr_ref[h : h + 1, :], st)
    pl.semaphore_wait(barrier, n_row - 1)

    def spread(count, to_of, src_of, dst, send_sem, recv_sem):
        def one(i, _):
            to = to_of(i)

            @pl.when(to != me)
            def _():
                pltpu.make_async_remote_copy(
                    src_ref=src_of(i), dst_ref=dst, send_sem=send_sem, recv_sem=recv_sem,
                    device_id=(to, col), device_id_type=MESH,
                ).start()

            @pl.when(to == me)
            def _():
                pltpu.make_async_copy(src_of(i), dst, recv_sem).start()
            return 0

        lax.fori_loop(0, count, one, 0)

    def worker_row(i):
        return (i // 8) * 16 + (i % 8) * 2

    def landed(ref, sem):
        pltpu.make_async_copy(ref, ref, sem).wait()

    spread(16, worker_row, lambda i: loss.at[i // 8], loss_all.at[me], loss_send, loss_recv)

    for h in range(2):
        part = slice(h * 128, (h + 1) * 128)
        c = cols[h]
        rs, tail = c[:, 0:1], c[:, 2:3]
        u = dot_left(inv[h] * wr_ref[h : h + 1, :], v_ref[:, part], NN)
        fresh[h] = u
        add[h] = dot_left(u * (tail * rs), x_ref[:, part], TN).astype(bf16)

    def block(ref):
        return lambda i: ref.at[i // 8, pl.ds(pl.multiple_of((i % 8) * 16, 16), 16), :]

    home = pl.ds(pl.multiple_of(slot * 16, 16), 16)
    spread(16, worker_row, block(add), got.at[me], s_send, s_recv)

    @pl.when(worker)
    def _():
        landed(loss_all, loss_recv)
        landed(got, s_recv)

        def step(i, s):
            s_low = s.astype(bf16)
            sent[i] = s_low
            return s - dot(s_low, loss_all[i], NN) + got[i].astype(f32)

        lax.fori_loop(0, n_row, step, jnp.zeros((16, 128), f32))
        spread(n_row, lambda i: i, lambda i: sent.at[i], state.at[head, home, :], b_send, b_recv)

    landed(state, b_recv)

    gain = gain_ref[0:1, :]
    for h in range(2):
        part = slice(h * 128, (h + 1) * 128)
        c = cols[h]
        decay = c[:, 1:2]
        s = state[h]
        u = fresh[h] - dot_left(carry[h], s, NT)
        fresh[h] = u
        raw = decay * dot(q_ref[:, part], s, NT) + dot_both(read[h], u, NN)
        r = lax.rsqrt(jnp.mean(raw * raw, axis=1, keepdims=True) + 1e-06)
        out_ref[:, part] = (raw * r * gain).astype(bf16)
        gg = og_ref[:, part].astype(f32) * gain
        d_raw = r * gg - raw * (r * r * r * jnp.mean(raw * gg, axis=1, keepdims=True))
        grad_raw[h] = d_raw
        z = dot_both(read[h], d_raw, TN)
        summed[h] = z
        add2[h] = (dot_left(decay * d_raw, q_ref[:, part], TN) - dot_both(z, carry[h], TN)).astype(bf16)

    spread(16, worker_row, block(add2), got2.at[me], t_send, t_recv)

    @pl.when(worker)
    def _():
        landed(got2, t_recv)

        def step(k, s):
            i = n_row - 1 - k
            s_low = s.astype(bf16)
            sent2[i] = s_low
            return s - dot(s_low, loss_all[i], NT) + got2[i].astype(f32)

        lax.fori_loop(0, n_row, step, jnp.zeros((16, 128), f32))
        spread(n_row, lambda i: i, lambda i: sent2.at[i], grad.at[head, home, :], u_send, u_recv)

    landed(grad, u_recv)

    n = 128
    rows_i = lax.broadcasted_iota(jnp.int32, (n, n), 0)
    cols_i = lax.broadcasted_iota(jnp.int32, (n, n), 1)
    for h in range(2):
        part = slice(h * 128, (h + 1) * 128)
        q, x = q_ref[:, part], x_ref[:, part]
        c = cols[h]
        rs, decay, tail, b = c[:, 0:1], c[:, 1:2], c[:, 2:3], c[:, 3:4]
        s, g, u, d_raw = state[h], grad[h], fresh[h], grad_raw[h]
        rs_row = jnp.sum(jnp.where(rows_i == cols_i, rs, 0.0), axis=0, keepdims=True)
        d_u = summed[h] + (tail * rs) * dot(x, g, NT)
        y = dot_both(inv[h], d_u, TN)
        dv_ref[:, part] = (b * y).astype(bf16)
        d_read = dot_both(d_raw, u, NT) * within[h]
        dq_ref[:, part] = (decay * dot_left(d_raw, s, NN) + dot_left(d_read * rs_row, x, NN)).astype(bf16)
        d_gram = jnp.where(rows_i > cols_i, -b * within[h] * dot_both(y, u, NT), 0.0)
        d_k = (
            dot_left(d_read, q, TN)
            + tail * dot_left(u, g, NN)
            - (b * decay) * dot_left(y, s, NN)
            + dot_left(d_gram * rs_row, x, NN)
            + dot_left(d_gram * rs, x, TN)
        )
        unit = rs * x.astype(f32)
        dk_ref[:, part] = (rs * (d_k - unit * jnp.sum(unit * d_k, axis=1, keepdims=True))).astype(bf16)

    def left(ref, sem):
        pltpu.make_async_copy(ref, ref, sem).wait()

    def drain(ref_block, count, sem):
        def one(i, _):
            pltpu.make_async_copy(ref_block, ref_block, sem).wait()
            return 0
        lax.fori_loop(0, count, one, 0)

    own = jnp.where(worker, 1, 0)
    drain(loss.at[0], 16 - own, loss_send)
    drain(got.at[0], 16 - own, s_send)
    drain(got2.at[0], 16 - own, t_send)

    @pl.when(worker)
    def _():
        drain(got.at[0], n_row - 1, b_send)
        drain(got2.at[0], n_row - 1, u_send)


def chain(v, q, x, og, ld, wr, gain):
    sq = (2, 128, 128)
    vm = pl.BlockSpec(memory_space=pltpu.VMEM)
    o = jax.ShapeDtypeStruct((128, 256), bf16)
    dma = pltpu.SemaphoreType.DMA
    return pl.pallas_call(
        chain_kernel,
        out_shape=(o, o, o, o),
        in_specs=[vm] * 7,
        out_specs=(vm,) * 4,
        scratch_shapes=[
            pltpu.VMEM(sq, f32), pltpu.VMEM(sq, f32), pltpu.VMEM(sq, f32), pltpu.VMEM(sq, f32),
            pltpu.VMEM(sq, f32), pltpu.VMEM(sq, bf16), pltpu.VMEM(sq, f32), pltpu.VMEM(sq, f32),
            pltpu.VMEM(sq, f32),
            pltpu.VMEM(sq, bf16), pltpu.VMEM(sq, bf16), pltpu.VMEM((32, 128, 128), bf16),
            pltpu.VMEM((32, 16, 128), bf16), pltpu.VMEM((32, 16, 128), bf16),
            pltpu.VMEM((32, 16, 128), bf16), pltpu.VMEM((32, 16, 128), bf16),
            pltpu.VMEM(sq, bf16), pltpu.VMEM(sq, bf16),
        ] + [dma] * 10,
        compiler_params=pltpu.CompilerParams(
            collective_id=1, has_side_effects=True, vmem_limit_bytes=40 * 1024 * 1024
        ),
        name="chain",
    )(v, q, x, og, ld, wr, gain)


def shards(
    activations, w_value, query_input, key_input, log_decay, write_rate, norm_gain, out_grad
):
    gathered = lax.all_gather(activations, "col", axis=1, tiled=True)
    weight_cols = lax.all_gather(w_value, "row", axis=0, tiled=True)
    value_sum = jnp.dot(gathered, weight_cols, preferred_element_type=jnp.float32)
    value_proj = value_sum.astype(jnp.bfloat16)
    chain_len = lax.axis_size("row")
    layer_out, d_query, d_key, d_value = chain(
        value_proj, query_input, key_input, out_grad, log_decay, write_rate,
        norm_gain.reshape(1, -1),
    )
    partials = lax.dot_general(
        d_value, weight_cols, (((1,), (1,)), ((), ())), preferred_element_type=jnp.float32
    )
    d_input = lax.psum_scatter(
        partials.astype(jnp.bfloat16), "col", scatter_dimension=1, tiled=True
    )
    weight_term = lax.dot_general(
        gathered, d_value, (((0,), (0,)), ((), ())), preferred_element_type=jnp.float32
    ).astype(jnp.bfloat16)
    owned_rows = w_value.shape[0]
    stacked = weight_term.reshape(chain_len, owned_rows, weight_term.shape[1])
    received = lax.all_to_all(stacked, "row", split_axis=0, concat_axis=0, tiled=True)
    d_w_value = jnp.sum(received.astype(jnp.float32), axis=0)
    return (layer_out, d_input, d_query, d_key, d_w_value)


def solution(mesh):
    in_specs = (
        P("row", "col"),
        P("row", "col"),
        P("row", "col"),
        P("row", "col"),
        P("col", "row"),
        P("col", "row"),
        P(),
        P("row", "col"),
    )
    out_specs = (
        P("row", "col"),
        P("row", "col"),
        P("row", "col"),
        P("row", "col"),
        P("row", "col"),
    )
    return jax.shard_map(shards, mesh=mesh, in_specs=in_specs, out_specs=out_specs, check_vma=False)
```

time: 929 us -> 483 us (0.52)
  starting transfers between devices: 260 us -> 7.51 us
  waiting for transfers between devices: 569 us -> 367 us
  Pallas kernels: 0 us -> 74.9 us
  matrix products: 41.6 us -> 9.81 us
  other arithmetic: 27.4 us -> 2.79 us
    ppermute x62 -> x0, waiting for transfers between devices: 297 us -> none  [passed_along(): lax.ppermute(value, axis, [(source, source + steps) for source in range(l...]
    ppermute x62 -> x0, starting transfers between devices: 253 us -> none  [passed_along(): lax.ppermute(value, axis, [(source, source + steps) for source in range(l...]
    pallas_call x0 -> x1, Pallas kernels: none -> 74.9 us  [chain(): pl.pallas_call(chain_kernel, out_shape=(o, o, o, o), in_specs=[vm] * 7, o...]
    all_to_all x1, waiting for transfers between devices: 83.1 us -> 150 us  [shards(): lax.all_to_all(stacked, 'row', split_axis=0, concat_axis=0, tiled=True)]
    dot_general x86 -> x0, matrix products: 29 us -> none  [the longest x31 8.5 us: relay_grad(): jnp.einsum('hvk,hkl->hvl', grad_now, flipped, precision=exact_mode)]
    all_gather x1, waiting for transfers between devices: 41.7 us -> 67.8 us  [shards(): gathered = lax.all_gather(activations, 'col', axis=1, tiled=True)]
    another operation x1 -> x0, other arithmetic: 19.7 us -> none  [block_terms(): solved = jax.scipy.linalg.solve_triangular(system, targets, lower=True)]
  transfers between devices with their start and end apart: 66 -> 4, of which waited for: 66 -> 3; matrix products, arithmetic and copies ran while one was open for 4% -> 2% of each run, Pallas kernels for 0% -> 0%
where the time goes in v1:
time: 483 us; the launch traced here: 481 us
  waiting for transfers between devices  367 us (76%)
  Pallas kernels  74.9 us (16%)
  between operations  13.9 us (3%)
  matrix products  9.81 us (2%)
  starting transfers between devices  7.51 us (2%)
  local copies, waits for them, and re-layouts  5.24 us (1%)
    all_to_all x1, waiting for transfers between devices, shards(): lax.all_to_all(stacked, 'row', split_axis=0, concat_axis=0, tiled=True)  150 us
    all_gather x1, waiting for transfers between devices, shards(): weight_cols = lax.all_gather(w_value, 'row', axis=0, tiled=True)  148 us
    pallas_call x1, Pallas kernels, chain(): pl.pallas_call(chain_kernel, out_shape=(o, o, o, o), in_specs=[vm] * 7, o...  74.9 us
    all_gather x1, waiting for transfers between devices, shards(): gathered = lax.all_gather(activations, 'col', axis=1, tiled=True)  67.8 us
  transfers between devices with their start and end apart: 4, of which 3 were waited for; matrix products, arithmetic and copies ran while one was open for 2% of the time, Pallas kernels for 0%

profile of v1, /device:TPU:6, one launch (start us, length us, event | category | flops | bytes accessed | tf_op | source)
XLA Modules:
  0.0 481.1 jit_solution(16013620705432668131)
XLA Ops:
  7.2 0.0 copy-start.2
  7.2 0.0 copy-start.5
  7.2 0.0 copy-start.4
  7.2 0.0 all-gather.3.cloned.1.call-start
  7.3 0.7 all-gather.3.cloned.1.call-update
  8.0 0.0 all-gather.5.cloned.1.call-start
  8.0 0.7 all-gather.5.cloned.1.call-update
  8.7 67.8 %all-gather.3.cloned.1.call-done = bf16[128,8192]{1,0:T(8,128)(2,1)} async-done(((bf16[128,512]{1,0:T(8,128)(2,1)}), bf16[128,8192]{1,0:T(8,128)(2,1)}) %all-gather.3.cloned.1.call-update) | async-done | bytes 2097168 | tf_op jit(solution)/shard_map/all_gather | solution.py:287
  76.5 148.1 %all-gather.5.cloned.1.call-done = bf16[8192,256]{1,0:T(8,128)(2,1)} async-done(((bf16[256,256]{1,0:T(8,128)(2,1)}), bf16[8192,256]{1,0:T(8,128)(2,1)}) %all-gather.5.cloned.1.call-update) | async-done | bytes 4194320 | tf_op jit(solution)/shard_map/all_gather | solution.py:288
  224.6 3.5 convolution_convert_fusion.2.v_ref
  228.2 74.9 %chain.1 = (bf16[128,256]{1,0:T(8,128)(2,1)S(1)}, bf16[128,256]{1,0:T(8,128)(2,1)S(1)}, bf16[128,256]{1,0:T(8,128)(2,1)S(1)}, bf16[128,256]{1,0:T(8,128)(2,1)S(1)}) custom-call(bf16[128,256]{1,0:T(8,128)(2,1)S(1)} %convolution_convert_fusion.2.v_ref, bf16[128,256]{1,0:T(8,128)(2,1)S(1)} %copy-done, bf16[128,256]{1,0:T(8,128)(2,1)S(1)} %copy-done.1, ...), custom_call_target="tpu_custom_call" | custom-call | tf_op jit(solution)/shard_map/chain/pallas_call | solution.py:263
  303.1 0.0 copy-done.6
  303.1 1.3 convolution_convert_fusion
  304.4 2.5 copy.19
  306.9 7.4 %all-to-all-start = ((bf16[32,256,256]{1,2,0:T(8,128)(2,1)}), bf16[32,256,256]{1,2,0:T(8,128)(2,1)}, u32[]{:S(2)}, u32[]{:S(2)}) async-start(bf16[32,256,256]{1,2,0:T(8,128)(2,1)} %bitcast.13), calls=%async_computation.1 | async-start | bytes 8388608 | tf_op jit(solution)/shard_map/all_to_all | solution.py:307
  314.3 0.0 reduce-scatter.2.cloned.1.call-start
  314.3 5.0 %convolution_convert_fusion.1 = bf16[128,8192]{1,0:T(8,128)(2,1)} fusion(bf16[128,256]{1,0:T(8,128)(2,1)S(1)} %get-tuple-element.10, bf16[8192,256]{1,0:T(8,128)(2,1)} %all-gather.5.cloned.1.call-done), kind=kOutput, calls=%fused_computation.1 | convolution fusion | flops 537919488 | bytes 6356992 | tf_op jit(solution)/shard_map/dot_general | solution.py:296
  319.3 0.0 reduce-scatter.2.cloned.1.call-update
  319.4 149.7 %all-to-all-done = bf16[32,256,256]{1,2,0:T(8,128)(2,1)} async-done(((bf16[32,256,256]{1,2,0:T(8,128)(2,1)}), bf16[32,256,256]{1,2,0:T(8,128)(2,1)}, u32[]{:S(2)}, u32[]{:S(2)}) %all-to-all-start) | async-done | bytes 4194336 | tf_op jit(solution)/shard_map/all_to_all | solution.py:307
  469.0 2.8 convert_reduce_fusion
  471.8 0.8 copy.15
  472.7 0.6 copy.23
  473.3 0.6 copy.24
  473.9 0.6 copy.25
  (11 shorter events, 0.0 us)
Async XLA Ops:
  7.2 221.0 %copy-start.2 = (bf16[128,256]{1,0:T(8,128)(2,1)S(1)}, bf16[128,256]{1,0:T(8,128)(2,1)}, u32[]{:S(2)}) copy-start(bf16[128,256]{1,0:T(8,128)(2,1)} %og_ref.1) | copy-start | bytes 196612
  7.2 221.0 %copy-start.5 = (f32[128]{0:T(128)S(1)}, f32[128]{0:T(128)}, u32[]{:S(2)}) copy-start(f32[128]{0:T(128)} %param.14) | copy-start | bytes 1540
  7.2 221.0 %copy-start.4 = (f32[2,128]{1,0:T(2,128)S(1)}, f32[2,128]{1,0:T(2,128)}, u32[]{:S(2)}) copy-start(f32[2,128]{1,0:T(2,128)} %wr_ref.1) | copy-start | bytes 3076
  7.2 221.0 %copy-start.3 = (f32[2,128]{1,0:T(2,128)S(1)}, f32[2,128]{1,0:T(2,128)}, u32[]{:S(2)}) copy-start(f32[2,128]{1,0:T(2,128)} %ld_ref.1) | copy-start | bytes 3076
  7.2 221.0 %copy-start.1 = (bf16[128,256]{1,0:T(8,128)(2,1)S(1)}, bf16[128,256]{1,0:T(8,128)(2,1)}, u32[]{:S(2)}) copy-start(bf16[128,256]{1,0:T(8,128)(2,1)} %x_ref.1) | copy-start | bytes 196612
  7.2 221.0 %copy-start = (bf16[128,256]{1,0:T(8,128)(2,1)S(1)}, bf16[128,256]{1,0:T(8,128)(2,1)}, u32[]{:S(2)}) copy-start(bf16[128,256]{1,0:T(8,128)(2,1)} %q_ref.1) | copy-start | bytes 196612
  7.2 69.3 %all-gather.3.cloned.1.call-start = ((), (), s32[]{:S(2)}) async-start(), calls=%async_computation.2 | async-start | bytes 2228224 | tf_op jit(solution)/shard_map/all_gather | solution.py:287
  8.0 216.7 %all-gather.5.cloned.1.call-start = ((), (), s32[]{:S(2)}) async-start(), calls=%async_computation.3 | async-start | bytes 4325376 | tf_op jit(solution)/shard_map/all_gather | solution.py:288
  76.5 226.6 %copy-start.6 = (bf16[128,8192]{1,0:T(8,128)(2,1)S(1)}, bf16[128,8192]{1,0:T(8,128)(2,1)}, u32[]{:S(2)}) copy-start(bf16[128,8192]{1,0:T(8,128)(2,1)} %all-gather.3.cloned.1.call-done) | copy-start | bytes 6291460
  306.9 162.2 %all-to-all-start = ((bf16[32,256,256]{1,2,0:T(8,128)(2,1)}), bf16[32,256,256]{1,2,0:T(8,128)(2,1)}, u32[]{:S(2)}, u32[]{:S(2)}) async-start(bf16[32,256,256]{1,2,0:T(8,128)(2,1)} %bitcast.13), calls=%async_computation.1 | async-start | bytes 8388608 | tf_op jit(solution)/shard_map/all_to_all | solution.py:307
  314.3 158.4 %reduce-scatter.2.cloned.1.call-start = ((), (), s32[]{:S(2)}) async-start(), calls=%async_computation.4 | async-start | bytes 2228224 | tf_op jit(solution)/shard_map/reduce_scatter | solution.py:299
Sparse Core Ops, SparseCore 0:
  11.3 65.1 all-gather.2
  78.6 145.9 all-gather.4
  320.5 96.0 reduce-scatter.1

commit v2 on v1

v2 whole, which is shorter than its diff:
```python
import functools

import jax
import jax.numpy as jnp
from jax import lax
from jax.experimental import pallas as pl
from jax.experimental.pallas import tpu as pltpu
from jax.sharding import PartitionSpec as P

MESH = pl.DeviceIdType.MESH
f32 = jnp.float32
bf16 = jnp.bfloat16
NN = (((1,), (0,)), ((), ()))
NT = (((1,), (1,)), ((), ()))
TN = (((0,), (0,)), ((), ()))


def dot(a, b, dims):
    return lax.dot_general(a, b, dims, preferred_element_type=f32)


def halves(a):
    high = a.astype(bf16)
    return high, (a - high.astype(f32)).astype(bf16)


def dot_left(a, b, dims):
    high, low = halves(a)
    return dot(high, b, dims) + dot(low, b, dims)


def dot_both(a, b, dims):
    a_high, a_low = halves(a)
    b_high, b_low = halves(b)
    return dot(a_high, b_high, dims) + (dot(a_high, b_low, dims) + dot(a_low, b_high, dims))


def key_terms(h, q, x, ld, wr, st):
    n = x.shape[0]
    rows = lax.broadcasted_iota(jnp.int32, (n, n), 0)
    cols = lax.broadcasted_iota(jnp.int32, (n, n), 1)
    lower = rows >= cols
    strict = rows > cols
    eye = rows == cols

    def col_of(row):
        return jnp.sum(jnp.where(eye, row, 0.0), axis=1, keepdims=True)

    def row_of(col):
        return jnp.sum(jnp.where(eye, col, 0.0), axis=0, keepdims=True)

    xf = x.astype(f32)
    rs = lax.rsqrt(jnp.sum(xf * xf, axis=1, keepdims=True) + 1e-06)
    rs_row = row_of(rs)
    g = jnp.sum(jnp.where(lower, ld, 0.0), axis=1, keepdims=True)
    g_row = row_of(g)
    total = jnp.sum(ld, axis=1, keepdims=True)
    decay = jnp.exp(g)
    decay_row = jnp.exp(g_row)
    tail = jnp.exp(total - g)
    b = col_of(wr)
    within = jnp.where(lower, jnp.exp(jnp.where(lower, g - g_row, 0.0)), 0.0)
    gram = dot(x, x, NT) * (rs * rs_row)
    coupling = jnp.where(strict, b * within * gram, 0.0)
    ident = jnp.where(eye, 1.0, 0.0)
    near = jnp.where((rows // 16) == (cols // 16), coupling, 0.0)
    inv = ident - near
    power = near
    yield
    for _ in range(3):
        power = dot_both(power, power, NN)
        inv = inv + dot_both(inv, power, NN)
        yield
    size = 16
    while size < n:
        off = ((rows // (2 * size)) == (cols // (2 * size))) & ((rows // size) != (cols // size))
        part = jnp.where(off, coupling, 0.0)
        inv = inv - dot_both(dot_both(inv, part, NN), inv, NN)
        size *= 2
        yield
    st["inv"][h] = inv
    st["within"][h] = within
    carry = dot_left(inv * (wr * decay_row * rs_row), x, NN)
    read = dot(q, x, NT) * within * rs_row
    loss = dot_left(carry * (tail * rs), x, TN) + jnp.where(eye, 1.0 - jnp.exp(total), 0.0)
    st["carry"][h] = carry
    st["read"][h] = read
    lanes = jnp.zeros((n, 128), f32)
    lane = lax.broadcasted_iota(jnp.int32, (n, 128), 1)
    for i, c in enumerate((rs, decay, tail, b)):
        lanes = jnp.where(lane == i, c, lanes)
    st["cols"][h] = lanes
    st["loss"][h] = loss.astype(bf16)


def layer_kernel(
    act_ref, w_ref, q_ref, x_ref, og_ref, ld_ref, wr_ref, gain_ref,
    out_ref, din_ref, dq_ref, dk_ref, dw_ref,
    inv, within, carry, read, cols, loss, fresh, grad_raw, summed, v_ref,
    act_own, act_all, w_all, part, part_in, loss_all,
    add, add2, got, got2, sent, sent2, state, grad,
    dv_all, w_terms, w_right, w_left, in_terms, in_sib, in_near, in_far, in_last,
    act_sem, act_sent, w_sem, w_sent, part_sem, loss_sem, loss_sent,
    s_send, s_recv, b_send, b_recv, t_send, t_recv, u_send, u_recv,
    dv_sem, r_sem, r_sent, i_sent, sib_sem, near_sem, far_sem, last_sem,
):
    n_row, n_z = 32, 16
    me, col = lax.axis_index("row"), lax.axis_index("col")
    a, z = me // n_z, me % n_z
    other = (1 - a) * n_z + z
    y, x_hi, core = col // 4, (col // 2) % 2, col % 2
    twin = col + 1 - 2 * core
    y_near = y + 1 - 2 * (y % 2)
    col_near = y_near * 4 + x_hi * 2 + core
    col_far = (3 - y) * 4 + x_hi * 2 + core
    source = a == y // 2
    first = jnp.where(source, y % 2, 1 - y % 2)
    slot = z // 2
    worker = z % 2 == 0
    up, down = a * n_z + (z + 1) % n_z, a * n_z + (z + n_z - 1) % n_z

    barrier = pltpu.get_barrier_semaphore()

    def greet(i, _):
        @pl.when(i != me)
        def _():
            pl.semaphore_signal(barrier, inc=1, device_id=(i, col), device_id_type=MESH)
        return 0

    lax.fori_loop(0, n_row, greet, 0)
    col_side = y * 4 + (1 - x_hi) * 2 + core
    for row_to, col_to in (
        (me, twin), (me, col_near), (me, col_far), (me, col_side), (other, col_side)
    ):
        pl.semaphore_signal(barrier, inc=1, device_id=(row_to, col_to), device_id_type=MESH)
    for i in range(2):
        act_own[i] = act_ref[:, i * 256 : (i + 1) * 256]
    pl.semaphore_wait(barrier, n_row - 1 + 5)

    def remote(src, dst, send_sem, recv_sem, row_to, col_to):
        pltpu.make_async_remote_copy(
            src_ref=src, dst_ref=dst, send_sem=send_sem, recv_sem=recv_sem,
            device_id=(row_to, col_to), device_id_type=MESH,
        ).start()

    def landed(ref, sem):
        pltpu.make_async_copy(ref, ref, sem).wait()

    home_row = (y // 2) * n_z + z
    for xh in range(2):
        to_col = y * 4 + xh * 2 + core
        here = source & (x_hi == xh)
        dst = act_all.at[a, col % 8]

        @pl.when(jnp.logical_not(here))
        def _():
            remote(act_own, dst, act_sent, act_sem.at[a, col % 8], home_row, to_col)

        @pl.when(here)
        def _():
            pltpu.make_async_copy(act_own, dst, act_sem.at[a, col % 8]).start()

    def act_first(i):
        t, xh = i // 2, i % 2
        cc = first * 4 + xh * 2 + core
        ref, sem = act_all.at[t, cc], act_sem.at[t, cc]
        landed(ref, sem)

        @pl.when(source)
        def _():
            remote(ref, ref, act_sent, sem, me, col_far)

        remote(ref, ref, act_sent, sem, me, col_near)
        remote(ref, ref, act_sent, sem, me, twin)

    def act_second(i):
        t, xh = i // 2, i % 2
        cc = (1 - first) * 4 + xh * 2 + core
        ref, sem = act_all.at[t, cc], act_sem.at[t, cc]
        landed(ref, sem)
        remote(ref, ref, act_sent, sem, me, twin)

    def act_last():
        for t in range(2):
            for k in range(4):
                cc = k * 2 + (1 - core)
                landed(act_all.at[t, cc], act_sem.at[t, cc])

    w_all[z] = w_ref[...]

    def w_piece(s, way, sub, origin):
        ref = w_all.at[origin, pl.ds(sub * 128, 128), :]
        return ref, w_sem.at[way, s, sub]

    def w_send(s, way):
        origin = (z + n_z - s) % n_z if way == 0 else (z + s) % n_z
        for sub in range(2):
            ref, sem = w_piece(s, way, sub, origin)
            remote(ref, ref, w_sent, sem, up if way == 0 else down, col)

    def w_step(s):
        for sub in range(2):
            for way in range(2):
                if way == 1 and s == 7:
                    continue
                origin = (z + n_z - s - 1) % n_z if way == 0 else (z + s + 1) % n_z
                ref, sem = w_piece(s, way, sub, origin)
                landed(ref, sem)
                if s + 1 < (8 if way == 0 else 7):
                    _, after = w_piece(s + 1, way, sub, origin)
                    remote(ref, ref, w_sent, after, up if way == 0 else down, col)

    w_send(0, 0)
    w_send(0, 1)

    def loss_start():
        loss_all[z, a] = loss[a]
        remote(loss.at[1 - a], loss_all.at[z, a], loss_sent.at[0], loss_sem.at[2, 0], other, col)

    def loss_first():
        landed(loss_all.at[z, 1 - a], loss_sem.at[2, 0])
        for way in range(2):
            remote(loss_all.at[z], loss_all.at[z], loss_sent.at[1], loss_sem.at[way, 0],
                   up if way == 0 else down, col)

    def loss_step(s):
        for way in range(2):
            if way == 1 and s == 7:
                continue
            origin = (z + n_z - s - 1) % n_z if way == 0 else (z + s + 1) % n_z
            landed(loss_all.at[origin], loss_sem.at[way, s])
            if s + 1 < (8 if way == 0 else 7):
                remote(loss_all.at[origin], loss_all.at[origin], loss_sent.at[1],
                       loss_sem.at[way, s + 1], up if way == 0 else down, col)

    st = dict(inv=inv, within=within, carry=carry, read=read, cols=cols, loss=loss)
    local = []
    for h in range(2):
        p = slice(h * 128, (h + 1) * 128)
        local.append(
            key_terms(h, q_ref[:, p], x_ref[:, p], ld_ref[h : h + 1, :], wr_ref[h : h + 1, :], st)
        )

    def think():
        for terms in local:
            next(terms, None)

    think()
    think()
    w_step(0)
    think()
    think()
    act_first(0)
    act_first(1)
    w_step(1)
    think()
    act_first(2)
    act_first(3)
    w_step(2)
    think()
    w_step(3)
    think()
    think()
    loss_start()
    w_step(4)
    act_second(0)
    act_second(1)
    loss_first()
    w_step(5)
    act_second(2)
    act_second(3)
    loss_step(0)
    w_step(6)
    loss_step(1)
    w_step(7)
    loss_step(2)
    act_last()
    loss_step(3)

    total = jnp.zeros((256, 256), f32)
    for k in range(n_z):
        both = jnp.concatenate([act_all[0, k // 2, k % 2], act_all[1, k // 2, k % 2]], axis=0)
        total = total + dot(both, w_all[k], NN)
    part[0] = total[:128]
    part[1] = total[128:]
    remote(part.at[1 - a], part_in, part_sem.at[0], part_sem.at[1], other, col)
    loss_step(4)
    landed(part_in, part_sem.at[1])
    v_ref[...] = (part[a] + part_in[...]).astype(bf16)
    loss_step(5)

    def spread(count, to_of, src_of, dst, send_sem, recv_sem):
        def one(i, _):
            to = to_of(i)

            @pl.when(to != me)
            def _():
                remote(src_of(i), dst, send_sem, recv_sem, to, col)

            @pl.when(to == me)
            def _():
                pltpu.make_async_copy(src_of(i), dst, recv_sem).start()
            return 0

        lax.fori_loop(0, count, one, 0)

    def worker_row(i):
        return (i // 8) * 16 + (i % 8) * 2

    for h in range(2):
        p = slice(h * 128, (h + 1) * 128)
        c = cols[h]
        rs, tail = c[:, 0:1], c[:, 2:3]
        u = dot_left(inv[h] * wr_ref[h : h + 1, :], v_ref[:, p], NN)
        fresh[h] = u
        add[h] = dot_left(u * (tail * rs), x_ref[:, p], TN).astype(bf16)

    def block(ref):
        return lambda i: ref.at[i // 8, pl.ds(pl.multiple_of((i % 8) * 16, 16), 16), :]

    home = pl.ds(pl.multiple_of(slot * 16, 16), 16)
    spread(16, worker_row, block(add), got.at[me], s_send, s_recv)
    loss_step(6)
    loss_step(7)

    @pl.when(worker)
    def _():
        landed(got, s_recv)

        def step(i, s):
            s_low = s.astype(bf16)
            sent[i] = s_low
            return s - dot(s_low, loss_all[i % 16, i // 16], NN) + got[i].astype(f32)

        lax.fori_loop(0, n_row, step, jnp.zeros((16, 128), f32))
        spread(n_row, lambda i: i, lambda i: sent.at[i], state.at[a, home, :], b_send, b_recv)

    landed(state, b_recv)

    gain = gain_ref[0:1, :]
    for h in range(2):
        p = slice(h * 128, (h + 1) * 128)
        c = cols[h]
        decay = c[:, 1:2]
        s = state[h]
        u = fresh[h] - dot_left(carry[h], s, NT)
        fresh[h] = u
        raw = decay * dot(q_ref[:, p], s, NT) + dot_both(read[h], u, NN)
        r = lax.rsqrt(jnp.mean(raw * raw, axis=1, keepdims=True) + 1e-06)
        out_ref[:, p] = (raw * r * gain).astype(bf16)
        gg = og_ref[:, p].astype(f32) * gain
        d_raw = r * gg - raw * (r * r * r * jnp.mean(raw * gg, axis=1, keepdims=True))
        grad_raw[h] = d_raw
        back = dot_both(read[h], d_raw, TN)
        summed[h] = back
        add2[h] = (dot_left(decay * d_raw, q_ref[:, p], TN) - dot_both(back, carry[h], TN)).astype(bf16)

    spread(16, worker_row, block(add2), got2.at[me], t_send, t_recv)

    @pl.when(worker)
    def _():
        landed(got2, t_recv)

        def step(k, s):
            i = n_row - 1 - k
            s_low = s.astype(bf16)
            sent2[i] = s_low
            return s - dot(s_low, loss_all[i % 16, i // 16], NT) + got2[i].astype(f32)

        lax.fori_loop(0, n_row, step, jnp.zeros((16, 128), f32))
        spread(n_row, lambda i: i, lambda i: sent2.at[i], grad.at[a, home, :], u_send, u_recv)

    landed(grad, u_recv)

    n = 128
    rows_i = lax.broadcasted_iota(jnp.int32, (n, n), 0)
    cols_i = lax.broadcasted_iota(jnp.int32, (n, n), 1)
    own_tokens = pl.ds(pl.multiple_of(a * 128, 128), 128)
    later = []
    for h in range(2):
        p = slice(h * 128, (h + 1) * 128)
        c = cols[h]
        rs, tail, b = c[:, 0:1], c[:, 2:3], c[:, 3:4]
        d_u = summed[h] + (tail * rs) * dot(x_ref[:, p], grad[h], NT)
        grown = dot_both(inv[h], d_u, TN)
        later.append(grown)
        dv_all[own_tokens, p] = (b * grown).astype(bf16)
    mine = dv_all.at[own_tokens, :]
    remote(mine, mine, dv_sem.at[0], dv_sem.at[1], other, col)

    def query_key_grads(h):
        p = slice(h * 128, (h + 1) * 128)
        q, x = q_ref[:, p], x_ref[:, p]
        c = cols[h]
        rs, decay, tail, b = c[:, 0:1], c[:, 1:2], c[:, 2:3], c[:, 3:4]
        s, g, u, d_raw, grown = state[h], grad[h], fresh[h], grad_raw[h], later[h]
        rs_row = jnp.sum(jnp.where(rows_i == cols_i, rs, 0.0), axis=0, keepdims=True)
        d_read = dot_both(d_raw, u, NT) * within[h]
        dq_ref[:, p] = (decay * dot_left(d_raw, s, NN) + dot_left(d_read * rs_row, x, NN)).astype(bf16)
        d_gram = jnp.where(rows_i > cols_i, -b * within[h] * dot_both(grown, u, NT), 0.0)
        d_k = (
            dot_left(d_read, q, TN)
            + tail * dot_left(u, g, NN)
            - (b * decay) * dot_left(grown, s, NN)
            + dot_left(d_gram * rs_row, x, NN)
            + dot_left(d_gram * rs, x, TN)
        )
        unit = rs * x.astype(f32)
        dk_ref[:, p] = (rs * (d_k - unit * jnp.sum(unit * d_k, axis=1, keepdims=True))).astype(bf16)

    theirs = dv_all.at[pl.ds(pl.multiple_of((1 - a) * 128, 128), 128), :]
    landed(theirs, dv_sem.at[1])

    def w_term(d):
        acc = dot(act_all[0, d // 2, d % 2], dv_all[0:128, :], TN)
        return acc + dot(act_all[1, d // 2, d % 2], dv_all[128:256, :], TN)

    def r_dest(s, way):
        return (z + 8 - s) % n_z if way == 0 else (z + n_z - 7 + s) % n_z

    def r_slot(s, way):
        return w_right.at[s] if way == 0 else w_left.at[s]

    def r_send(s, way):
        d = r_dest(s, way)
        for sub in range(2):
            q = pl.ds(sub * 128, 128)
            if s > 0:
                landed(r_slot(s - 1, way).at[q, :], r_sem.at[way, s - 1, sub])
                w_terms[d, q, :] = (
                    w_terms[d, q, :].astype(f32) + r_slot(s - 1, way)[q, :].astype(f32)
                ).astype(bf16)
            remote(w_terms.at[d, q, :], r_slot(s, way).at[q, :], r_sent, r_sem.at[way, s, sub],
                   up if way == 0 else down, col)

    def r_make(s):
        for way in range(2):
            if way == 1 and s == 7:
                continue
            d = r_dest(s, way)
            w_terms[d] = w_term(d).astype(bf16)

    def r_step(s):
        for way in range(2):
            if way == 1 and s == 7:
                continue
            r_send(s, way)

    def in_make(cc):
        for i in range(2):
            both = dot(dv_all[...], w_all[cc * 2 + i], NT).astype(bf16)
            for t in range(2):
                in_terms[t, cc, i] = both[t * 128 : (t + 1) * 128]

    def plus(t, cc, ref):
        in_terms[t, cc] = (in_terms[t, cc].astype(f32) + ref[...].astype(f32)).astype(bf16)

    def sib_send(k):
        cc = k * 2 + 1 - core
        in_make(cc)
        for t in range(2):
            remote(in_terms.at[t, cc], in_sib.at[t, k], i_sent, sib_sem.at[t, k], me, twin)

    def own_make(k):
        in_make(k * 2 + core)

    def near_send(i):
        t, xh = i // 2, i % 2
        k = (1 - first) * 2 + xh
        cc = k * 2 + core
        landed(in_sib.at[t, k], sib_sem.at[t, k])
        plus(t, cc, in_sib.at[t, k])
        remote(in_terms.at[t, cc], in_near.at[t, xh], i_sent, near_sem.at[t, xh], me, col_near)

    def far_send(i):
        t, xh = i // 2, i % 2
        k = first * 2 + xh
        cc = k * 2 + core
        landed(in_sib.at[t, k], sib_sem.at[t, k])
        plus(t, cc, in_sib.at[t, k])
        landed(in_near.at[t, xh], near_sem.at[t, xh])
        plus(t, cc, in_near.at[t, xh])

        @pl.when(jnp.logical_not(source))
        def _():
            remote(in_terms.at[t, cc], in_far.at[t, xh], i_sent, far_sem.at[t, xh], me, col_far)

    def home_send(i):
        t, xh = i // 2, i % 2
        k = first * 2 + xh
        cc = k * 2 + core

        @pl.when(source)
        def _():
            landed(in_far.at[t, xh], far_sem.at[t, xh])
            plus(t, cc, in_far.at[t, xh])
            row_to, col_to = t * n_z + z, y * 4 + xh * 2 + core
            here = (row_to == me) & (col_to == col)

            @pl.when(jnp.logical_not(here))
            def _():
                remote(in_terms.at[t, cc], in_last.at[x_hi], i_sent, last_sem.at[x_hi], row_to, col_to)

            @pl.when(here)
            def _():
                pltpu.make_async_copy(in_terms.at[t, cc], in_last.at[x_hi], last_sem.at[x_hi]).start()

    r_make(0)
    r_step(0)
    for k in range(4):
        sib_send(k)
    r_make(1)
    for k in range(4):
        own_make(k)
    r_step(1)
    r_make(2)
    near_send(0)
    near_send(1)
    near_send(2)
    near_send(3)
    r_step(2)
    r_make(3)
    query_key_grads(0)
    r_step(3)
    r_make(4)
    far_send(0)
    far_send(1)
    r_step(4)
    r_make(5)
    far_send(2)
    far_send(3)
    query_key_grads(1)
    r_step(5)
    r_make(6)
    home_send(0)
    home_send(1)
    r_step(6)
    r_make(7)
    home_send(2)
    home_send(3)
    r_step(7)
    own_term = w_term(z)
    for xh in range(2):
        landed(in_last.at[xh], last_sem.at[xh])
    for i in range(2):
        din_ref[:, i * 256 : (i + 1) * 256] = (
            in_last[0, i].astype(f32) + in_last[1, i].astype(f32)
        ).astype(bf16)
    for sub in range(2):
        q = pl.ds(sub * 128, 128)
        landed(w_right.at[7, q, :], r_sem.at[0, 7, sub])
        landed(w_left.at[6, q, :], r_sem.at[1, 6, sub])
    dw_ref[...] = own_term + w_right[7].astype(f32) + w_left[6].astype(f32)

    def drain(ref, count, sem):
        def one(i, _):
            pltpu.make_async_copy(ref, ref, sem).wait()
            return 0
        lax.fori_loop(0, count, one, 0)

    big = act_own
    own = jnp.where(worker, 1, 0)
    far = jnp.where(source, 1, 0)
    self_home = jnp.where(source, 1, 0)
    drain(big, 2 - self_home + 4 + 4 * far + 8, act_sent)
    drain(w_all.at[0, pl.ds(0, 128), :], 30, w_sent)
    landed(part.at[0], part_sem.at[0])
    landed(loss.at[0], loss_sent.at[0])
    drain(loss_all.at[0], 15, loss_sent.at[1])
    drain(got.at[0], 16 - own, s_send)
    drain(got.at[0], 16 - own, t_send)

    @pl.when(worker)
    def _():
        drain(got.at[0], n_row - 1, b_send)
        drain(got.at[0], n_row - 1, u_send)

    landed(mine, dv_sem.at[0])
    drain(w_all.at[0, pl.ds(0, 128), :], 30, r_sent)
    drain(big, 8 + 4 + 4 * (1 - far) + (4 - 1) * far, i_sent)


def layer(act, w, q, x, og, ld, wr, gain):
    sq = (2, 128, 128)
    vm = pl.BlockSpec(memory_space=pltpu.VMEM)
    o = jax.ShapeDtypeStruct((128, 256), bf16)
    dma = pltpu.SemaphoreType.DMA
    V = pltpu.VMEM
    return pl.pallas_call(
        layer_kernel,
        out_shape=(
            o,
            jax.ShapeDtypeStruct((128, 512), bf16),
            o,
            o,
            jax.ShapeDtypeStruct((256, 256), f32),
        ),
        in_specs=[vm] * 8,
        out_specs=(vm,) * 5,
        scratch_shapes=[
            V(sq, f32), V(sq, f32), V(sq, f32), V(sq, f32), V(sq, f32), V(sq, bf16),
            V(sq, f32), V(sq, f32), V(sq, f32), V((128, 256), bf16),
            V((2, 128, 256), bf16), V((2, 8, 2, 128, 256), bf16), V((16, 256, 256), bf16),
            V((2, 128, 256), f32), V((128, 256), f32), V((16, 2, 128, 128), bf16),
            V(sq, bf16), V(sq, bf16), V((32, 16, 128), bf16), V((32, 16, 128), bf16),
            V((32, 16, 128), bf16), V((32, 16, 128), bf16), V(sq, bf16), V(sq, bf16),
            V((256, 256), bf16), V((16, 256, 256), bf16), V((8, 256, 256), bf16),
            V((7, 256, 256), bf16), V((2, 8, 2, 128, 256), bf16), V((2, 4, 2, 128, 256), bf16),
            V((2, 2, 2, 128, 256), bf16), V((2, 2, 2, 128, 256), bf16), V((2, 2, 128, 256), bf16),
            dma((2, 8)), dma, dma((2, 8, 2)), dma, dma((2,)), dma((3, 8)), dma((2,)),
            dma, dma, dma, dma, dma, dma, dma, dma,
            dma((2,)), dma((2, 8, 2)), dma, dma, dma((2, 4)), dma((2, 2)), dma((2, 2)), dma((2,)),
        ],
        compiler_params=pltpu.CompilerParams(
            collective_id=1, has_side_effects=True, vmem_limit_bytes=48 * 1024 * 1024
        ),
        name="layer",
    )(act, w, q, x, og, ld, wr, gain)


def shards(
    activations, w_value, query_input, key_input, log_decay, write_rate, norm_gain, out_grad
):
    return layer(
        activations, w_value, query_input, key_input, out_grad, log_decay, write_rate,
        norm_gain.reshape(1, -1),
    )


def solution(mesh):
    split = P("row", "col")
    flipped = P("col", "row")
    return jax.shard_map(
        shards,
        mesh=mesh,
        in_specs=(split, split, split, split, flipped, flipped, P(), split),
        out_specs=(split,) * 5,
        check_vma=False,
    )
```

time: 483 us -> 163 us (0.34)
  waiting for transfers between devices: 367 us -> 0 us
  Pallas kernels: 74.9 us -> 151 us
  between operations: 13.9 us -> 0.67 us
  matrix products: 9.81 us -> 0 us
  starting transfers between devices: 7.51 us -> 0 us
    all_gather x2 -> x0, waiting for transfers between devices: 216 us -> none  [the longest x1 148 us: shards(): weight_cols = lax.all_gather(w_value, 'row', axis=0, tiled=True)]
    all_to_all x1 -> x0, waiting for transfers between devices: 150 us -> none  [shards(): lax.all_to_all(stacked, 'row', split_axis=0, concat_axis=0, tiled=True)]
    pallas_call x1, Pallas kernels: 74.9 us -> 151 us  [layer(): pl.pallas_call(layer_kernel, out_shape=(o, jax.ShapeDtypeStruct((128, 512...]
    dot_general x3 -> x0, matrix products: 9.81 us -> none  [the longest x1 5.01 us: shards(): lax.dot_general(d_value, weight_cols, (((1,), (1,)), ((), ())), preferred...]
    all_to_all x1 -> x0, starting transfers between devices: 7.4 us -> none  [shards(): lax.all_to_all(stacked, 'row', split_axis=0, concat_axis=0, tiled=True)]
    unnamed x18 -> x21, local copies, waits for them, and re-layouts: 2.75 us -> 8.93 us
  transfers between devices with their start and end apart: 4 -> 0, of which waited for: 3 -> 0; matrix products, arithmetic and copies ran while one was open for 2% -> 0% of each run, Pallas kernels for 0% -> 0%
where the time goes in v2:
time: 163 us; the launch traced here: 161 us
  Pallas kernels  151 us (93%)
  local copies, waits for them, and re-layouts  8.93 us (5%)
    pallas_call x1, Pallas kernels, layer(): pl.pallas_call(layer_kernel, out_shape=(o, jax.ShapeDtypeStruct((128, 512...  151 us
    unnamed x21, local copies, waits for them, and re-layouts  8.93 us

profile of v2, /device:TPU:6, one launch (start us, length us, event | category | flops | bytes accessed | tf_op | source)
XLA Modules:
  0.0 161.1 jit_solution(3533282966216803035)
XLA Ops:
  0.6 0.0 copy-start.7
  0.6 0.0 copy-start.5
  0.7 0.6 copy-done.7
  1.3 0.0 copy-done.5
  1.3 0.0 copy-start
  1.3 0.9 copy-done
  2.2 0.0 copy-start.1
  2.2 0.9 copy-done.1
  3.1 0.0 copy-start.2
  3.1 0.8 copy-done.2
  4.0 0.0 copy-start.3
  4.0 0.8 copy-done.3
  4.8 0.0 copy-start.4
  4.8 0.8 copy-done.4
  5.7 0.0 copy-start.6
  5.7 0.7 copy-done.6
  6.3 151.5 %layer.1 = (bf16[128,256]{1,0:T(8,128)(2,1)S(1)}, bf16[128,512]{1,0:T(8,128)(2,1)S(1)}, bf16[128,256]{1,0:T(8,128)(2,1)S(1)}, bf16[128,256]{1,0:T(8,128)(2,1)S(1)}, f32[256,256]{1,0:T(8,128)S(1)}) custom-call(bf16[128,512]{1,0:T(8,128)(2,1)S(1)} %copy-done, bf16[256,256]{1,0:T(8,128)(2,1)S(1)} %copy-done.1, bf16[128,256]{1,0:T(8,128)(2,1)S(1)} %copy-done.2, ...), custom_call_target="tpu_custom_call" | custom-call | tf_op jit(solution)/shard_map/layer/pallas_call | solution.py:589
  157.8 0.6 copy.18
  158.5 0.7 copy.19
  159.1 0.6 copy.20
  159.8 0.6 copy.21
  160.4 0.7 copy.22
Async XLA Ops:
  0.6 0.7 copy-start.7
  0.6 0.7 copy-start.5
  1.3 0.9 copy-start
  2.2 0.9 copy-start.1
  3.1 0.8 copy-start.2
  4.0 0.8 copy-start.3
  4.8 0.8 copy-start.4
  5.7 0.7 copy-start.6

commit v3 on v2

--- a/solution.py
+++ b/solution.py
@@ -93,8 +93,13 @@
     st["loss"][h] = loss.astype(bf16)
 
 
+SUBS = 4
+UNROLL = 4
+SUB = 256 // SUBS
+
+
 def layer_kernel(
-    act_ref, w_ref, q_ref, x_ref, og_ref, ld_ref, wr_ref, gain_ref,
+    act_hbm, w_hbm, q_hbm, x_hbm, og_hbm, ld_hbm, wr_hbm, gain_hbm,
     out_ref, din_ref, dq_ref, dk_ref, dw_ref,
     inv, within, carry, read, cols, loss, fresh, grad_raw, summed, v_ref,
     act_own, act_all, w_all, part, part_in, loss_all,
@@ -103,6 +108,7 @@
     act_sem, act_sent, w_sem, w_sent, part_sem, loss_sem, loss_sent,
     s_send, s_recv, b_send, b_recv, t_send, t_recv, u_send, u_recv,
     dv_sem, r_sem, r_sent, i_sent, sib_sem, near_sem, far_sem, last_sem,
+    q_ref, x_ref, og_ref, ld_ref, wr_ref, gain_ref, load_sem,
 ):
     n_row, n_z = 32, 16
     me, col = lax.axis_index("row"), lax.axis_index("col")
@@ -121,21 +127,29 @@
 
     barrier = pltpu.get_barrier_semaphore()
 
-    def greet(i, _):
-        @pl.when(i != me)
-        def _():
-            pl.semaphore_signal(barrier, inc=1, device_id=(i, col), device_id_type=MESH)
-        return 0
-
-    lax.fori_loop(0, n_row, greet, 0)
     col_side = y * 4 + (1 - x_hi) * 2 + core
     for row_to, col_to in (
-        (me, twin), (me, col_near), (me, col_far), (me, col_side), (other, col_side)
+        (up, col), (down, col), (other, col), (me, twin), (me, col_near), (me, col_far),
+        (me, col_side), (other, col_side),
     ):
         pl.semaphore_signal(barrier, inc=1, device_id=(row_to, col_to), device_id_type=MESH)
-    for i in range(2):
-        act_own[i] = act_ref[:, i * 256 : (i + 1) * 256]
-    pl.semaphore_wait(barrier, n_row - 1 + 5)
+    w_own = w_all.at[z]
+    loads = [
+        pltpu.make_async_copy(act_hbm.at[:, pl.ds(i * 256, 256)], act_own.at[i], load_sem.at[i])
+        for i in range(2)
+    ] + [pltpu.make_async_copy(w_hbm, w_own, load_sem.at[2])]
+    more = [
+        pltpu.make_async_copy(src, dst, load_sem.at[3 + i])
+        for i, (src, dst) in enumerate((
+            (q_hbm, q_ref), (x_hbm, x_ref), (og_hbm, og_ref), (ld_hbm, ld_ref), (wr_hbm, wr_ref),
+            (gain_hbm, gain_ref),
+        ))
+    ]
+    for load in loads + more:
+        load.start()
+    for load in loads:
+        load.wait()
+    pl.semaphore_wait(barrier, 8)
 
     def remote(src, dst, send_sem, recv_sem, row_to, col_to):
         pltpu.make_async_remote_copy(
@@ -150,20 +164,21 @@
     for xh in range(2):
         to_col = y * 4 + xh * 2 + core
         here = source & (x_hi == xh)
-        dst = act_all.at[a, col % 8]
-
-        @pl.when(jnp.logical_not(here))
-        def _():
-            remote(act_own, dst, act_sent, act_sem.at[a, col % 8], home_row, to_col)
-
-        @pl.when(here)
-        def _():
-            pltpu.make_async_copy(act_own, dst, act_sem.at[a, col % 8]).start()
+        for f in range(2):
+            dst, sem = act_all.at[a, col % 8, f], act_sem.at[a, col % 8, f]
+
+            @pl.when(jnp.logical_not(here))
+            def _():
+                remote(act_own.at[f], dst, act_sent, sem, home_row, to_col)
+
+            @pl.when(here)
+            def _():
+                pltpu.make_async_copy(act_own.at[f], dst, sem).start()
 
     def act_first(i):
-        t, xh = i // 2, i % 2
+        t, xh, f = i // 4, (i // 2) % 2, i % 2
         cc = first * 4 + xh * 2 + core
-        ref, sem = act_all.at[t, cc], act_sem.at[t, cc]
+        ref, sem = act_all.at[t, cc, f], act_sem.at[t, cc, f]
         landed(ref, sem)
 
         @pl.when(source)
@@ -174,9 +189,9 @@
         remote(ref, ref, act_sent, sem, me, twin)
 
     def act_second(i):
-        t, xh = i // 2, i % 2
+        t, xh, f = i // 4, (i // 2) % 2, i % 2
         cc = (1 - first) * 4 + xh * 2 + core
-        ref, sem = act_all.at[t, cc], act_sem.at[t, cc]
+        ref, sem = act_all.at[t, cc, f], act_sem.at[t, cc, f]
         landed(ref, sem)
         remote(ref, ref, act_sent, sem, me, twin)
 
@@ -184,22 +199,21 @@
         for t in range(2):
             for k in range(4):
                 cc = k * 2 + (1 - core)
-                landed(act_all.at[t, cc], act_sem.at[t, cc])
-
-    w_all[z] = w_ref[...]
+                for f in range(2):
+                    landed(act_all.at[t, cc, f], act_sem.at[t, cc, f])
 
     def w_piece(s, way, sub, origin):
-        ref = w_all.at[origin, pl.ds(sub * 128, 128), :]
+        ref = w_all.at[origin, pl.ds(sub * SUB, SUB), :]
         return ref, w_sem.at[way, s, sub]
 
     def w_send(s, way):
         origin = (z + n_z - s) % n_z if way == 0 else (z + s) % n_z
-        for sub in range(2):
+        for sub in range(SUBS):
             ref, sem = w_piece(s, way, sub, origin)
             remote(ref, ref, w_sent, sem, up if way == 0 else down, col)
 
     def w_step(s):
-        for sub in range(2):
+        for sub in range(SUBS):
             for way in range(2):
                 if way == 1 and s == 7:
                     continue
@@ -234,6 +248,8 @@
                        loss_sem.at[way, s + 1], up if way == 0 else down, col)
 
     st = dict(inv=inv, within=within, carry=carry, read=read, cols=cols, loss=loss)
+    for load in more:
+        load.wait()
     local = []
     for h in range(2):
         p = slice(h * 128, (h + 1) * 128)
@@ -250,12 +266,12 @@
     w_step(0)
     think()
     think()
-    act_first(0)
-    act_first(1)
+    for i in range(4):
+        act_first(i)
     w_step(1)
     think()
-    act_first(2)
-    act_first(3)
+    for i in range(4, 8):
+        act_first(i)
     w_step(2)
     think()
     w_step(3)
@@ -263,12 +279,12 @@
     think()
     loss_start()
     w_step(4)
-    act_second(0)
-    act_second(1)
+    for i in range(4):
+        act_second(i)
     loss_first()
     w_step(5)
-    act_second(2)
-    act_second(3)
+    for i in range(4, 8):
+        act_second(i)
     loss_step(0)
     w_step(6)
     loss_step(1)
@@ -289,23 +305,30 @@
     v_ref[...] = (part[a] + part_in[...]).astype(bf16)
     loss_step(5)
 
-    def spread(count, to_of, src_of, dst, send_sem, recv_sem):
-        def one(i, _):
-            to = to_of(i)
-
-            @pl.when(to != me)
-            def _():
-                remote(src_of(i), dst, send_sem, recv_sem, to, col)
-
-            @pl.when(to == me)
-            def _():
-                pltpu.make_async_copy(src_of(i), dst, recv_sem).start()
-            return 0
-
-        lax.fori_loop(0, count, one, 0)
-
-    def worker_row(i):
-        return (i // 8) * 16 + (i % 8) * 2
+    lane_rows = pl.ds(pl.multiple_of(slot * 16, 16), 16)
+
+    def deal(src, dst, send_sem, recv_sem):
+        for j in range(16):
+            k = (a * 8 + slot + j) % 16
+            block = src.at[k // 8, pl.ds(pl.multiple_of((k % 8) * 16, 16), 16), :]
+            to = (k // 8) * n_z + (k % 8) * 2
+            if j:
+                remote(block, dst.at[me], send_sem, recv_sem, to, col)
+            else:
+                @pl.when(worker)
+                def _():
+                    pltpu.make_async_copy(block, dst.at[me], recv_sem).start()
+
+                @pl.when(jnp.logical_not(worker))
+                def _():
+                    remote(block, dst.at[me], send_sem, recv_sem, to, col)
+
+    def give_back(i, src, dst, send_sem, recv_sem):
+        mine = i == me
+        remote(
+            src.at[i], dst.at[jnp.where(mine, 2, a), lane_rows, :], send_sem, recv_sem,
+            jnp.where(mine, other, i), col,
+        )
 
     for h in range(2):
         p = slice(h * 128, (h + 1) * 128)
@@ -315,11 +338,7 @@
         fresh[h] = u
         add[h] = dot_left(u * (tail * rs), x_ref[:, p], TN).astype(bf16)
 
-    def block(ref):
-        return lambda i: ref.at[i // 8, pl.ds(pl.multiple_of((i % 8) * 16, 16), 16), :]
-
-    home = pl.ds(pl.multiple_of(slot * 16, 16), 16)
-    spread(16, worker_row, block(add), got.at[me], s_send, s_recv)
+    deal(add, got, s_send, s_recv)
     loss_step(6)
     loss_step(7)
 
@@ -330,12 +349,13 @@
         def step(i, s):
             s_low = s.astype(bf16)
             sent[i] = s_low
+            give_back(i, sent, state, b_send, b_recv)
             return s - dot(s_low, loss_all[i % 16, i // 16], NN) + got[i].astype(f32)
 
-        lax.fori_loop(0, n_row, step, jnp.zeros((16, 128), f32))
-        spread(n_row, lambda i: i, lambda i: sent.at[i], state.at[a, home, :], b_send, b_recv)
-
-    landed(state, b_recv)
+        lax.fori_loop(0, n_row, step, jnp.zeros((16, 128), f32), unroll=UNROLL)
+        state[a, lane_rows, :] = sent[me]
+
+    landed(state.at[pl.ds(0, 2)], b_recv)
 
     gain = gain_ref[0:1, :]
     for h in range(2):
@@ -355,7 +375,7 @@
         summed[h] = back
         add2[h] = (dot_left(decay * d_raw, q_ref[:, p], TN) - dot_both(back, carry[h], TN)).astype(bf16)
 
-    spread(16, worker_row, block(add2), got2.at[me], t_send, t_recv)
+    deal(add2, got2, t_send, t_recv)
 
     @pl.when(worker)
     def _():
@@ -365,12 +385,13 @@
             i = n_row - 1 - k
             s_low = s.astype(bf16)
             sent2[i] = s_low
+            give_back(i, sent2, grad, u_send, u_recv)
             return s - dot(s_low, loss_all[i % 16, i // 16], NT) + got2[i].astype(f32)
 
-        lax.fori_loop(0, n_row, step, jnp.zeros((16, 128), f32))
-        spread(n_row, lambda i: i, lambda i: sent2.at[i], grad.at[a, home, :], u_send, u_recv)
-
-    landed(grad, u_recv)
+        lax.fori_loop(0, n_row, step, jnp.zeros((16, 128), f32), unroll=UNROLL)
+        grad[a, lane_rows, :] = sent2[me]
+
+    landed(grad.at[pl.ds(0, 2)], u_recv)
 
     n = 128
     rows_i = lax.broadcasted_iota(jnp.int32, (n, n), 0)
@@ -423,8 +444,8 @@
 
     def r_send(s, way):
         d = r_dest(s, way)
-        for sub in range(2):
-            q = pl.ds(sub * 128, 128)
+        for sub in range(SUBS):
+            q = pl.ds(sub * SUB, SUB)
             if s > 0:
                 landed(r_slot(s - 1, way).at[q, :], r_sem.at[way, s - 1, sub])
                 w_terms[d, q, :] = (
@@ -452,58 +473,60 @@
             for t in range(2):
                 in_terms[t, cc, i] = both[t * 128 : (t + 1) * 128]
 
-    def plus(t, cc, ref):
-        in_terms[t, cc] = (in_terms[t, cc].astype(f32) + ref[...].astype(f32)).astype(bf16)
+    def plus(t, cc, f, ref):
+        in_terms[t, cc, f] = (in_terms[t, cc, f].astype(f32) + ref[...].astype(f32)).astype(bf16)
 
     def sib_send(k):
         cc = k * 2 + 1 - core
         in_make(cc)
         for t in range(2):
-            remote(in_terms.at[t, cc], in_sib.at[t, k], i_sent, sib_sem.at[t, k], me, twin)
+            for f in range(2):
+                remote(in_terms.at[t, cc, f], in_sib.at[t, k, f], i_sent, sib_sem.at[t, k, f], me, twin)
 
     def own_make(k):
         in_make(k * 2 + core)
 
     def near_send(i):
-        t, xh = i // 2, i % 2
+        t, xh, f = i // 4, (i // 2) % 2, i % 2
         k = (1 - first) * 2 + xh
         cc = k * 2 + core
-        landed(in_sib.at[t, k], sib_sem.at[t, k])
-        plus(t, cc, in_sib.at[t, k])
-        remote(in_terms.at[t, cc], in_near.at[t, xh], i_sent, near_sem.at[t, xh], me, col_near)
+        landed(in_sib.at[t, k, f], sib_sem.at[t, k, f])
+        plus(t, cc, f, in_sib.at[t, k, f])
+        remote(in_terms.at[t, cc, f], in_near.at[t, xh, f], i_sent, near_sem.at[t, xh, f], me, col_near)
 
     def far_send(i):
-        t, xh = i // 2, i % 2
+        t, xh, f = i // 4, (i // 2) % 2, i % 2
         k = first * 2 + xh
         cc = k * 2 + core
-        landed(in_sib.at[t, k], sib_sem.at[t, k])
-        plus(t, cc, in_sib.at[t, k])
-        landed(in_near.at[t, xh], near_sem.at[t, xh])
-        plus(t, cc, in_near.at[t, xh])
+        landed(in_sib.at[t, k, f], sib_sem.at[t, k, f])
+        plus(t, cc, f, in_sib.at[t, k, f])
+        landed(in_near.at[t, xh, f], near_sem.at[t, xh, f])
+        plus(t, cc, f, in_near.at[t, xh, f])
 
         @pl.when(jnp.logical_not(source))
         def _():
-            remote(in_terms.at[t, cc], in_far.at[t, xh], i_sent, far_sem.at[t, xh], me, col_far)
+            remote(in_terms.at[t, cc, f], in_far.at[t, xh, f], i_sent, far_sem.at[t, xh, f], me, col_far)
 
     def home_send(i):
-        t, xh = i // 2, i % 2
+        t, xh, f = i // 4, (i // 2) % 2, i % 2
         k = first * 2 + xh
         cc = k * 2 + core
 
         @pl.when(source)
         def _():
-            landed(in_far.at[t, xh], far_sem.at[t, xh])
-            plus(t, cc, in_far.at[t, xh])
+            landed(in_far.at[t, xh, f], far_sem.at[t, xh, f])
+            plus(t, cc, f, in_far.at[t, xh, f])
             row_to, col_to = t * n_z + z, y * 4 + xh * 2 + core
             here = (row_to == me) & (col_to == col)
+            dst, sem = in_last.at[x_hi, f], last_sem.at[x_hi, f]
 
             @pl.when(jnp.logical_not(here))
             def _():
-                remote(in_terms.at[t, cc], in_last.at[x_hi], i_sent, last_sem.at[x_hi], row_to, col_to)
+                remote(in_terms.at[t, cc, f], dst, i_sent, sem, row_to, col_to)
 
             @pl.when(here)
             def _():
-                pltpu.make_async_copy(in_terms.at[t, cc], in_last.at[x_hi], last_sem.at[x_hi]).start()
+                pltpu.make_async_copy(in_terms.at[t, cc, f], dst, sem).start()
 
     r_make(0)
     r_step(0)
@@ -514,40 +537,41 @@
         own_make(k)
     r_step(1)
     r_make(2)
-    near_send(0)
-    near_send(1)
-    near_send(2)
-    near_send(3)
+    for i in range(4):
+        near_send(i)
     r_step(2)
+    for i in range(4, 8):
+        near_send(i)
     r_make(3)
     query_key_grads(0)
     r_step(3)
     r_make(4)
-    far_send(0)
-    far_send(1)
+    for i in range(4):
+        far_send(i)
     r_step(4)
     r_make(5)
-    far_send(2)
-    far_send(3)
+    for i in range(4, 8):
+        far_send(i)
     query_key_grads(1)
     r_step(5)
     r_make(6)
-    home_send(0)
-    home_send(1)
+    for i in range(4):
+        home_send(i)
     r_step(6)
     r_make(7)
-    home_send(2)
-    home_send(3)
+    for i in range(4, 8):
+        home_send(i)
     r_step(7)
     own_term = w_term(z)
     for xh in range(2):
-        landed(in_last.at[xh], last_sem.at[xh])
+        for f in range(2):
+            landed(in_last.at[xh, f], last_sem.at[xh, f])
     for i in range(2):
         din_ref[:, i * 256 : (i + 1) * 256] = (
             in_last[0, i].astype(f32) + in_last[1, i].astype(f32)
         ).astype(bf16)
-    for sub in range(2):
-        q = pl.ds(sub * 128, 128)
+    for sub in range(SUBS):
+        q = pl.ds(sub * SUB, SUB)
         landed(w_right.at[7, q, :], r_sem.at[0, 7, sub])
         landed(w_left.at[6, q, :], r_sem.at[1, 6, sub])
     dw_ref[...] = own_term + w_right[7].astype(f32) + w_left[6].astype(f32)
@@ -558,12 +582,12 @@
             return 0
         lax.fori_loop(0, count, one, 0)
 
-    big = act_own
+    big = act_own.at[0]
     own = jnp.where(worker, 1, 0)
     far = jnp.where(source, 1, 0)
     self_home = jnp.where(source, 1, 0)
-    drain(big, 2 - self_home + 4 + 4 * far + 8, act_sent)
-    drain(w_all.at[0, pl.ds(0, 128), :], 30, w_sent)
+    drain(big, (2 - self_home + 4 + 4 * far + 8) * 2, act_sent)
+    drain(w_all.at[0, pl.ds(0, SUB), :], 15 * SUBS, w_sent)
     landed(part.at[0], part_sem.at[0])
     landed(loss.at[0], loss_sent.at[0])
     drain(loss_all.at[0], 15, loss_sent.at[1])
@@ -572,12 +596,12 @@
 
     @pl.when(worker)
     def _():
-        drain(got.at[0], n_row - 1, b_send)
-        drain(got.at[0], n_row - 1, u_send)
+        drain(got.at[0], n_row, b_send)
+        drain(got.at[0], n_row, u_send)
 
     landed(mine, dv_sem.at[0])
-    drain(w_all.at[0, pl.ds(0, 128), :], 30, r_sent)
-    drain(big, 8 + 4 + 4 * (1 - far) + (4 - 1) * far, i_sent)
+    drain(w_all.at[0, pl.ds(0, SUB), :], 15 * SUBS, r_sent)
+    drain(big, (8 + 4 + 4 * (1 - far) + (4 - 1) * far) * 2, i_sent)
 
 
 def layer(act, w, q, x, og, ld, wr, gain):
@@ -595,7 +619,7 @@
             o,
             jax.ShapeDtypeStruct((256, 256), f32),
         ),
-        in_specs=[vm] * 8,
+        in_specs=[pl.BlockSpec(memory_space=pl.ANY)] * 8,
         out_specs=(vm,) * 5,
         scratch_shapes=[
             V(sq, f32), V(sq, f32), V(sq, f32), V(sq, f32), V(sq, f32), V(sq, bf16),
@@ -603,13 +627,15 @@
             V((2, 128, 256), bf16), V((2, 8, 2, 128, 256), bf16), V((16, 256, 256), bf16),
             V((2, 128, 256), f32), V((128, 256), f32), V((16, 2, 128, 128), bf16),
             V(sq, bf16), V(sq, bf16), V((32, 16, 128), bf16), V((32, 16, 128), bf16),
-            V((32, 16, 128), bf16), V((32, 16, 128), bf16), V(sq, bf16), V(sq, bf16),
+            V((32, 16, 128), bf16), V((32, 16, 128), bf16), V((3, 128, 128), bf16), V((3, 128, 128), bf16),
             V((256, 256), bf16), V((16, 256, 256), bf16), V((8, 256, 256), bf16),
             V((7, 256, 256), bf16), V((2, 8, 2, 128, 256), bf16), V((2, 4, 2, 128, 256), bf16),
             V((2, 2, 2, 128, 256), bf16), V((2, 2, 2, 128, 256), bf16), V((2, 2, 128, 256), bf16),
-            dma((2, 8)), dma, dma((2, 8, 2)), dma, dma((2,)), dma((3, 8)), dma((2,)),
+            dma((2, 8, 2)), dma, dma((2, 8, SUBS)), dma, dma((2,)), dma((3, 8)), dma((2,)),
             dma, dma, dma, dma, dma, dma, dma, dma,
-            dma((2,)), dma((2, 8, 2)), dma, dma, dma((2, 4)), dma((2, 2)), dma((2, 2)), dma((2,)),
+            dma((2,)), dma((2, 8, SUBS)), dma, dma, dma((2, 4, 2)), dma((2, 2, 2)), dma((2, 2, 2)), dma((2, 2)),
+            V((128, 256), bf16), V((128, 256), bf16), V((128, 256), bf16), V((2, 128), f32),
+            V((2, 128), f32), V((1, 128), f32), dma((9,)),
         ],
         compiler_params=pltpu.CompilerParams(
             collective_id=1, has_side_effects=True, vmem_limit_bytes=48 * 1024 * 1024

time: 163 us -> 154 us (0.945)
  Pallas kernels: 151 us -> 144 us
    pallas_call x1, Pallas kernels: 151 us -> 144 us  [layer(): pl.pallas_call(layer_kernel, out_shape=(o, jax.ShapeDtypeStruct((128, 512...]
where the time goes in v3:
time: 154 us; the launch traced here: 153 us
  Pallas kernels  144 us (94%)
  local copies, waits for them, and re-layouts  8.93 us (6%)
    pallas_call x1, Pallas kernels, layer(): pl.pallas_call(layer_kernel, out_shape=(o, jax.ShapeDtypeStruct((128, 512...  144 us
    unnamed x21, local copies, waits for them, and re-layouts  8.93 us

profile of v3, /device:TPU:6, one launch (start us, length us, event | category | flops | bytes accessed | tf_op | source)
XLA Modules:
  0.0 153.4 jit_solution(5480468592732538036)
XLA Ops:
  0.6 0.0 copy-start.7
  0.6 0.0 copy-start.5
  0.7 0.6 copy-done.7
  1.3 0.0 copy-done.5
  1.3 0.0 copy-start
  1.3 0.9 copy-done
  2.2 0.0 copy-start.1
  2.2 0.9 copy-done.1
  3.1 0.0 copy-start.2
  3.1 0.8 copy-done.2
  4.0 0.0 copy-start.3
  4.0 0.8 copy-done.3
  4.8 0.0 copy-start.4
  4.8 0.8 copy-done.4
  5.7 0.0 copy-start.6
  5.7 0.7 copy-done.6
  6.3 143.8 %layer.1 = (bf16[128,256]{1,0:T(8,128)(2,1)S(1)}, bf16[128,512]{1,0:T(8,128)(2,1)S(1)}, bf16[128,256]{1,0:T(8,128)(2,1)S(1)}, bf16[128,256]{1,0:T(8,128)(2,1)S(1)}, f32[256,256]{1,0:T(8,128)S(1)}) custom-call(bf16[128,512]{1,0:T(8,128)(2,1)S(1)} %copy-done, bf16[256,256]{1,0:T(8,128)(2,1)S(1)} %copy-done.1, bf16[128,256]{1,0:T(8,128)(2,1)S(1)} %copy-done.2, ...), custom_call_target="tpu_custom_call" | custom-call | tf_op jit(solution)/shard_map/layer/pallas_call | solution.py:613
  150.1 0.6 copy.18
  150.8 0.7 copy.19
  151.4 0.6 copy.20
  152.0 0.6 copy.21
  152.7 0.7 copy.22
Async XLA Ops:
  0.6 0.7 copy-start.7
  0.6 0.7 copy-start.5
  1.3 0.9 copy-start
  2.2 0.9 copy-start.1
  3.1 0.8 copy-start.2
  4.0 0.8 copy-start.3
  4.8 0.8 copy-start.4
  5.7 0.7 copy-start.6

commit v4 on v3

--- a/solution.py
+++ b/solution.py
@@ -95,7 +95,15 @@
 
 SUBS = 4
 UNROLL = 4
+FIRST = 3
+ORDER = (
+    "t", "w0", "a0123", "t", "w1", "a4567", "t", "t", "t", "s", "w2", "c01", "b01", "p",
+    "w3", "b234", "c234", "l0", "w4", "b567", "c567", "l1", "w5", "d0123", "l2",
+    "w6", "d4567", "l3", "w7", "x", "l4",
+)
 SUB = 256 // SUBS
+R_SUBS = 4
+R_SUB = 256 // R_SUBS
 
 
 def layer_kernel(
@@ -145,8 +153,25 @@
             (gain_hbm, gain_ref),
         ))
     ]
-    for load in loads + more:
+    for load in more + loads:
         load.start()
+
+    st = dict(inv=inv, within=within, carry=carry, read=read, cols=cols, loss=loss)
+    for load in more:
+        load.wait()
+    local = []
+    for h in range(2):
+        p = slice(h * 128, (h + 1) * 128)
+        local.append(
+            key_terms(h, q_ref[:, p], x_ref[:, p], ld_ref[h : h + 1, :], wr_ref[h : h + 1, :], st)
+        )
+
+    def think():
+        for terms in local:
+            next(terms, None)
+
+    for _ in range(FIRST):
+        think()
     for load in loads:
         load.wait()
     pl.semaphore_wait(barrier, 8)
@@ -175,16 +200,14 @@
             def _():
                 pltpu.make_async_copy(act_own.at[f], dst, sem).start()
 
-    def act_first(i):
+    def act_first(i, is_source):
         t, xh, f = i // 4, (i // 2) % 2, i % 2
         cc = first * 4 + xh * 2 + core
         ref, sem = act_all.at[t, cc, f], act_sem.at[t, cc, f]
         landed(ref, sem)
 
-        @pl.when(source)
-        def _():
+        if is_source:
             remote(ref, ref, act_sent, sem, me, col_far)
-
         remote(ref, ref, act_sent, sem, me, col_near)
         remote(ref, ref, act_sent, sem, me, twin)
 
@@ -227,71 +250,66 @@
     w_send(0, 0)
     w_send(0, 1)
 
+    def loss_send(k, s):
+        for way in range(2):
+            if s >= (8 if way == 0 else 7):
+                continue
+            origin = (z + n_z - s) % n_z if way == 0 else (z + s) % n_z
+            owner = a if k == 0 else 1 - a
+            ref = loss_all.at[origin, owner]
+            remote(ref, ref, loss_sent.at[1], loss_sem.at[way, s, owner], up if way == 0 else down, col)
+
     def loss_start():
+        remote(loss.at[1 - a], loss_all.at[z, a], loss_sent.at[0], loss_sem.at[2, 0, 0], other, col)
         loss_all[z, a] = loss[a]
-        remote(loss.at[1 - a], loss_all.at[z, a], loss_sent.at[0], loss_sem.at[2, 0], other, col)
+        loss_send(0, 0)
 
     def loss_first():
-        landed(loss_all.at[z, 1 - a], loss_sem.at[2, 0])
-        for way in range(2):
-            remote(loss_all.at[z], loss_all.at[z], loss_sent.at[1], loss_sem.at[way, 0],
-                   up if way == 0 else down, col)
+        landed(loss_all.at[z, 1 - a], loss_sem.at[2, 0, 0])
+        loss_send(1, 0)
 
     def loss_step(s):
-        for way in range(2):
-            if way == 1 and s == 7:
-                continue
-            origin = (z + n_z - s - 1) % n_z if way == 0 else (z + s + 1) % n_z
-            landed(loss_all.at[origin], loss_sem.at[way, s])
-            if s + 1 < (8 if way == 0 else 7):
-                remote(loss_all.at[origin], loss_all.at[origin], loss_sent.at[1],
-                       loss_sem.at[way, s + 1], up if way == 0 else down, col)
-
-    st = dict(inv=inv, within=within, carry=carry, read=read, cols=cols, loss=loss)
-    for load in more:
-        load.wait()
-    local = []
-    for h in range(2):
-        p = slice(h * 128, (h + 1) * 128)
-        local.append(
-            key_terms(h, q_ref[:, p], x_ref[:, p], ld_ref[h : h + 1, :], wr_ref[h : h + 1, :], st)
-        )
-
-    def think():
-        for terms in local:
-            next(terms, None)
-
-    think()
-    think()
-    w_step(0)
-    think()
-    think()
-    for i in range(4):
-        act_first(i)
-    w_step(1)
-    think()
-    for i in range(4, 8):
-        act_first(i)
-    w_step(2)
-    think()
-    w_step(3)
-    think()
-    think()
-    loss_start()
-    w_step(4)
-    for i in range(4):
-        act_second(i)
-    loss_first()
-    w_step(5)
-    for i in range(4, 8):
-        act_second(i)
-    loss_step(0)
-    w_step(6)
-    loss_step(1)
-    w_step(7)
-    loss_step(2)
-    act_last()
-    loss_step(3)
+        for k in range(2):
+            owner = a if k == 0 else 1 - a
+            for way in range(2):
+                if way == 1 and s == 7:
+                    continue
+                origin = (z + n_z - s - 1) % n_z if way == 0 else (z + s + 1) % n_z
+                landed(loss_all.at[origin, owner], loss_sem.at[way, s, owner])
+            loss_send(k, s + 1)
+
+    def at_source(work):
+        pl.when(source)(work)
+
+    def at_sink(work):
+        pl.when(jnp.logical_not(source))(work)
+
+    def each(work, numbers, *rest):
+        for number in numbers:
+            work(int(number), *rest)
+
+    for item in ORDER:
+        what, number = item[0], item[1:]
+        if what == "t":
+            think()
+        elif what == "w":
+            w_step(int(number))
+        elif what == "a":
+            at_source(functools.partial(each, act_first, number, True))
+        elif what == "b":
+            at_sink(functools.partial(each, act_first, number, False))
+        elif what == "c":
+            at_source(functools.partial(each, act_second, number))
+        elif what == "d":
+            at_sink(functools.partial(each, act_second, number))
+        elif what == "s":
+            loss_start()
+        elif what == "p":
+            loss_first()
+        elif what == "l":
+            loss_step(int(number))
+        elif what == "x":
+            act_last()
 
     total = jnp.zeros((256, 256), f32)
     for k in range(n_z):
@@ -300,7 +318,6 @@
     part[0] = total[:128]
     part[1] = total[128:]
     remote(part.at[1 - a], part_in, part_sem.at[0], part_sem.at[1], other, col)
-    loss_step(4)
     landed(part_in, part_sem.at[1])
     v_ref[...] = (part[a] + part_in[...]).astype(bf16)
     loss_step(5)
@@ -308,20 +325,20 @@
     lane_rows = pl.ds(pl.multiple_of(slot * 16, 16), 16)
 
     def deal(src, dst, send_sem, recv_sem):
-        for j in range(16):
-            k = (a * 8 + slot + j) % 16
+        for j in (4, 12, 5, 13, 3, 11, 6, 14, 2, 10, 7, 15, 1, 9, 8, 0):
+            k = (1 - a + j // 8) % 2 * 8 + (slot + j) % 8
             block = src.at[k // 8, pl.ds(pl.multiple_of((k % 8) * 16, 16), 16), :]
             to = (k // 8) * n_z + (k % 8) * 2
-            if j:
-                remote(block, dst.at[me], send_sem, recv_sem, to, col)
+            if j != 8:
+                remote(block, dst.at[me], send_sem, recv_sem.at[me], to, col)
             else:
                 @pl.when(worker)
                 def _():
-                    pltpu.make_async_copy(block, dst.at[me], recv_sem).start()
+                    pltpu.make_async_copy(block, dst.at[me], recv_sem.at[me]).start()
 
                 @pl.when(jnp.logical_not(worker))
                 def _():
-                    remote(block, dst.at[me], send_sem, recv_sem, to, col)
+                    remote(block, dst.at[me], send_sem, recv_sem.at[me], to, col)
 
     def give_back(i, src, dst, send_sem, recv_sem):
         mine = i == me
@@ -344,12 +361,11 @@
 
     @pl.when(worker)
     def _():
-        landed(got, s_recv)
-
         def step(i, s):
             s_low = s.astype(bf16)
             sent[i] = s_low
             give_back(i, sent, state, b_send, b_recv)
+            landed(got.at[i], s_recv.at[i])
             return s - dot(s_low, loss_all[i % 16, i // 16], NN) + got[i].astype(f32)
 
         lax.fori_loop(0, n_row, step, jnp.zeros((16, 128), f32), unroll=UNROLL)
@@ -379,13 +395,12 @@
 
     @pl.when(worker)
     def _():
-        landed(got2, t_recv)
-
         def step(k, s):
             i = n_row - 1 - k
             s_low = s.astype(bf16)
             sent2[i] = s_low
             give_back(i, sent2, grad, u_send, u_recv)
+            landed(got2.at[i], t_recv.at[i])
             return s - dot(s_low, loss_all[i % 16, i // 16], NT) + got2[i].astype(f32)
 
         lax.fori_loop(0, n_row, step, jnp.zeros((16, 128), f32), unroll=UNROLL)
@@ -444,8 +459,8 @@
 
     def r_send(s, way):
         d = r_dest(s, way)
-        for sub in range(SUBS):
-            q = pl.ds(sub * SUB, SUB)
+        for sub in range(R_SUBS):
+            q = pl.ds(sub * R_SUB, R_SUB)
             if s > 0:
                 landed(r_slot(s - 1, way).at[q, :], r_sem.at[way, s - 1, sub])
                 w_terms[d, q, :] = (
@@ -570,8 +585,8 @@
         din_ref[:, i * 256 : (i + 1) * 256] = (
             in_last[0, i].astype(f32) + in_last[1, i].astype(f32)
         ).astype(bf16)
-    for sub in range(SUBS):
-        q = pl.ds(sub * SUB, SUB)
+    for sub in range(R_SUBS):
+        q = pl.ds(sub * R_SUB, R_SUB)
         landed(w_right.at[7, q, :], r_sem.at[0, 7, sub])
         landed(w_left.at[6, q, :], r_sem.at[1, 6, sub])
     dw_ref[...] = own_term + w_right[7].astype(f32) + w_left[6].astype(f32)
@@ -590,7 +605,7 @@
     drain(w_all.at[0, pl.ds(0, SUB), :], 15 * SUBS, w_sent)
     landed(part.at[0], part_sem.at[0])
     landed(loss.at[0], loss_sent.at[0])
-    drain(loss_all.at[0], 15, loss_sent.at[1])
+    drain(loss.at[0], 30, loss_sent.at[1])
     drain(got.at[0], 16 - own, s_send)
     drain(got.at[0], 16 - own, t_send)
 
@@ -600,7 +615,7 @@
         drain(got.at[0], n_row, u_send)
 
     landed(mine, dv_sem.at[0])
-    drain(w_all.at[0, pl.ds(0, SUB), :], 15 * SUBS, r_sent)
+    drain(w_all.at[0, pl.ds(0, R_SUB), :], 15 * R_SUBS, r_sent)
     drain(big, (8 + 4 + 4 * (1 - far) + (4 - 1) * far) * 2, i_sent)
 
 
@@ -619,7 +634,7 @@
             o,
             jax.ShapeDtypeStruct((256, 256), f32),
         ),
-        in_specs=[pl.BlockSpec(memory_space=pl.ANY)] * 8,
+        in_specs=[pl.BlockSpec(memory_space=pltpu.HBM)] * 8,
         out_specs=(vm,) * 5,
         scratch_shapes=[
             V(sq, f32), V(sq, f32), V(sq, f32), V(sq, f32), V(sq, f32), V(sq, bf16),
@@ -631,14 +646,14 @@
             V((256, 256), bf16), V((16, 256, 256), bf16), V((8, 256, 256), bf16),
             V((7, 256, 256), bf16), V((2, 8, 2, 128, 256), bf16), V((2, 4, 2, 128, 256), bf16),
             V((2, 2, 2, 128, 256), bf16), V((2, 2, 2, 128, 256), bf16), V((2, 2, 128, 256), bf16),
-            dma((2, 8, 2)), dma, dma((2, 8, SUBS)), dma, dma((2,)), dma((3, 8)), dma((2,)),
-            dma, dma, dma, dma, dma, dma, dma, dma,
-            dma((2,)), dma((2, 8, SUBS)), dma, dma, dma((2, 4, 2)), dma((2, 2, 2)), dma((2, 2, 2)), dma((2, 2)),
+            dma((2, 8, 2)), dma, dma((2, 8, SUBS)), dma, dma((2,)), dma((3, 8, 2)), dma((2,)),
+            dma, dma((32,)), dma, dma, dma, dma((32,)), dma, dma,
+            dma((2,)), dma((2, 8, R_SUBS)), dma, dma, dma((2, 4, 2)), dma((2, 2, 2)), dma((2, 2, 2)), dma((2, 2)),
             V((128, 256), bf16), V((128, 256), bf16), V((128, 256), bf16), V((2, 128), f32),
             V((2, 128), f32), V((1, 128), f32), dma((9,)),
         ],
         compiler_params=pltpu.CompilerParams(
-            collective_id=1, has_side_effects=True, vmem_limit_bytes=48 * 1024 * 1024
+            collective_id=1, has_side_effects=True, vmem_limit_bytes=63 * 1024 * 1024
         ),
         name="layer",
     )(act, w, q, x, og, ld, wr, gain)

time: 154 us -> 133 us (0.86)
  Pallas kernels: 144 us -> 127 us
  local copies, waits for them, and re-layouts: 8.93 us -> 4.37 us
    pallas_call x1, Pallas kernels: 144 us -> 127 us  [layer(): pl.pallas_call(layer_kernel, out_shape=(o, jax.ShapeDtypeStruct((128, 512...]
    unnamed x21 -> x13, local copies, waits for them, and re-layouts: 8.93 us -> 4.37 us
where the time goes in v4:
time: 133 us; the launch traced here: 132 us
  Pallas kernels  127 us (95%)
  local copies, waits for them, and re-layouts  4.37 us (3%)
    pallas_call x1, Pallas kernels, layer(): pl.pallas_call(layer_kernel, out_shape=(o, jax.ShapeDtypeStruct((128, 512...  127 us
    unnamed x13, local copies, waits for them, and re-layouts  4.37 us

profile of v4, /device:TPU:6, one launch (start us, length us, event | category | flops | bytes accessed | tf_op | source)
XLA Modules:
  0.0 132.4 jit_solution(11244137618545921985)
XLA Ops:
  0.6 127.4 %layer.1 = (bf16[128,256]{1,0:T(8,128)(2,1)}, bf16[128,512]{1,0:T(8,128)(2,1)}, bf16[128,256]{1,0:T(8,128)(2,1)}, bf16[128,256]{1,0:T(8,128)(2,1)}, f32[256,256]{1,0:T(8,128)}) custom-call(bf16[128,512]{1,0:T(8,128)(2,1)} %act_hbm.1, bf16[256,256]{1,0:T(8,128)(2,1)} %w_hbm.1, bf16[128,256]{1,0:T(8,128)(2,1)} %q_hbm.1, bf16[128,256]{1,0:T(8,128)(2,1)} %x_hbm.1, ...), custom_call_target="tpu_custom_call" | custom-call | tf_op jit(solution)/shard_map/layer/pallas_call | solution.py:628
  128.0 0.0 copy-start.1
  128.0 0.0 copy-start.3
  128.0 1.5 %copy.18 = bf16[128,256]{1,0:T(8,128)(2,1)} copy(bf16[128,256]{1,0:T(8,128)(2,1)} %get-tuple-element.10) | data formatting | bytes 131072
  129.6 0.0 copy-done.1
  129.6 0.0 copy-start
  129.6 0.7 copy.19
  130.2 0.0 copy-done.3
  130.2 0.0 copy-start.2
  130.2 0.6 copy.20
  130.9 0.2 copy-done.2
  131.1 0.6 copy.21
  131.7 0.0 copy-done
  131.7 0.7 copy.22
Async XLA Ops:
  128.0 1.5 %copy-start.1 = (bf16[128,512]{1,0:T(8,128)(2,1)S(1)}, bf16[128,512]{1,0:T(8,128)(2,1)}, u32[]{:S(2)}) copy-start(bf16[128,512]{1,0:T(8,128)(2,1)} %get-tuple-element.11) | copy-start | bytes 393220
  128.0 2.2 %copy-start.3 = (bf16[128,256]{1,0:T(8,128)(2,1)S(1)}, bf16[128,256]{1,0:T(8,128)(2,1)}, u32[]{:S(2)}) copy-start(bf16[128,256]{1,0:T(8,128)(2,1)} %get-tuple-element.12) | copy-start | bytes 196612
  129.6 2.2 %copy-start = (f32[256,256]{1,0:T(8,128)S(1)}, f32[256,256]{1,0:T(8,128)}, u32[]{:S(2)}) copy-start(f32[256,256]{1,0:T(8,128)} %get-tuple-element.14) | copy-start | bytes 786436
  130.2 0.9 copy-start.2

commit v5 on v4

--- a/solution.py
+++ b/solution.py
@@ -99,7 +99,7 @@
 ORDER = (
     "t", "w0", "a0123", "t", "w1", "a4567", "t", "t", "t", "s", "w2", "c01", "b01", "p",
     "w3", "b234", "c234", "l0", "w4", "b567", "c567", "l1", "w5", "d0123", "l2",
-    "w6", "d4567", "l3", "w7", "x", "l4",
+    "w6", "d4567", "l3", "w7", "x",
 )
 SUB = 256 // SUBS
 R_SUBS = 4
@@ -116,7 +116,7 @@
     act_sem, act_sent, w_sem, w_sent, part_sem, loss_sem, loss_sent,
     s_send, s_recv, b_send, b_recv, t_send, t_recv, u_send, u_recv,
     dv_sem, r_sem, r_sent, i_sent, sib_sem, near_sem, far_sem, last_sem,
-    q_ref, x_ref, og_ref, ld_ref, wr_ref, gain_ref, load_sem,
+    q_ref, x_ref, og_ref, ld_ref, wr_ref, gain_ref, load_sem, loss_turned,
 ):
     n_row, n_z = 32, 16
     me, col = lax.axis_index("row"), lax.axis_index("col")
@@ -318,6 +318,7 @@
     part[0] = total[:128]
     part[1] = total[128:]
     remote(part.at[1 - a], part_in, part_sem.at[0], part_sem.at[1], other, col)
+    loss_step(4)
     landed(part_in, part_sem.at[1])
     v_ref[...] = (part[a] + part_in[...]).astype(bf16)
     loss_step(5)
@@ -370,6 +371,12 @@
 
         lax.fori_loop(0, n_row, step, jnp.zeros((16, 128), f32), unroll=UNROLL)
         state[a, lane_rows, :] = sent[me]
+
+        def turn(i, _):
+            loss_turned[i] = loss_all[i % 16, i // 16].T
+            return 0
+
+        lax.fori_loop(0, n_row, turn, 0, unroll=UNROLL)
 
     landed(state.at[pl.ds(0, 2)], b_recv)
 
@@ -401,7 +408,7 @@
             sent2[i] = s_low
             give_back(i, sent2, grad, u_send, u_recv)
             landed(got2.at[i], t_recv.at[i])
-            return s - dot(s_low, loss_all[i % 16, i // 16], NT) + got2[i].astype(f32)
+            return s - dot(s_low, loss_turned[i], NN) + got2[i].astype(f32)
 
         lax.fori_loop(0, n_row, step, jnp.zeros((16, 128), f32), unroll=UNROLL)
         grad[a, lane_rows, :] = sent2[me]
@@ -650,7 +657,7 @@
             dma, dma((32,)), dma, dma, dma, dma((32,)), dma, dma,
             dma((2,)), dma((2, 8, R_SUBS)), dma, dma, dma((2, 4, 2)), dma((2, 2, 2)), dma((2, 2, 2)), dma((2, 2)),
             V((128, 256), bf16), V((128, 256), bf16), V((128, 256), bf16), V((2, 128), f32),
-            V((2, 128), f32), V((1, 128), f32), dma((9,)),
+            V((2, 128), f32), V((1, 128), f32), dma((9,)), V((32, 128, 128), bf16),
         ],
         compiler_params=pltpu.CompilerParams(
             collective_id=1, has_side_effects=True, vmem_limit_bytes=63 * 1024 * 1024
@@ -659,13 +666,26 @@
     )(act, w, q, x, og, ld, wr, gain)
 
 
+def finish_kernel(*refs):
+    for src, dst in zip(refs[:5], refs[5:]):
+        dst[...] = src[...]
+
+
+def finished(results):
+    return pl.pallas_call(
+        finish_kernel,
+        out_shape=tuple(jax.ShapeDtypeStruct(r.shape, r.dtype) for r in results),
+        name="finish",
+    )(*results)
+
+
 def shards(
     activations, w_value, query_input, key_input, log_decay, write_rate, norm_gain, out_grad
 ):
-    return layer(
+    return finished(layer(
         activations, w_value, query_input, key_input, out_grad, log_decay, write_rate,
         norm_gain.reshape(1, -1),
-    )
+    ))
 
 
 def solution(mesh):

time: 133 us -> 129 us (0.970)
  local copies, waits for them, and re-layouts: 4.37 us -> 0 us
    unnamed x13 -> x0, local copies, waits for them, and re-layouts: 4.37 us -> none
    pallas_call x1, Pallas kernels: 127 us -> 125 us  [layer(): pl.pallas_call(layer_kernel, out_shape=(o, jax.ShapeDtypeStruct((128, 512...]
    pallas_call x0 -> x1, Pallas kernels: none -> 1.94 us  [finished(): pl.pallas_call(finish_kernel, out_shape=tuple((jax.ShapeDtypeStruct(r.sha...]
where the time goes in v5:
time: 129 us; the launch traced here: 128 us
  Pallas kernels  127 us (98%)
    pallas_call x1, Pallas kernels, layer(): pl.pallas_call(layer_kernel, out_shape=(o, jax.ShapeDtypeStruct((128, 512...  125 us

profile of v5, /device:TPU:6, one launch (start us, length us, event | category | flops | bytes accessed | tf_op | source)
XLA Modules:
  0.0 127.9 jit_solution(7900249127870930386)
XLA Ops:
  0.6 125.3 %layer.1 = (bf16[128,256]{1,0:T(8,128)(2,1)}, bf16[128,512]{1,0:T(8,128)(2,1)}, bf16[128,256]{1,0:T(8,128)(2,1)}, bf16[128,256]{1,0:T(8,128)(2,1)}, f32[256,256]{1,0:T(8,128)}) custom-call(bf16[128,512]{1,0:T(8,128)(2,1)} %act_hbm.1, bf16[256,256]{1,0:T(8,128)(2,1)} %w_hbm.1, bf16[128,256]{1,0:T(8,128)(2,1)} %q_hbm.1, bf16[128,256]{1,0:T(8,128)(2,1)} %x_hbm.1, ...), custom_call_target="tpu_custom_call" | custom-call | tf_op jit(solution)/shard_map/layer/pallas_call | solution.py:635
  126.0 1.9 %finish.1 = (bf16[128,256]{1,0:T(8,128)(2,1)}, bf16[128,512]{1,0:T(8,128)(2,1)}, bf16[128,256]{1,0:T(8,128)(2,1)}, bf16[128,256]{1,0:T(8,128)(2,1)}, f32[256,256]{1,0:T(8,128)}) custom-call(bf16[128,256]{1,0:T(8,128)(2,1)} %get-tuple-element.10.refs_0_, bf16[128,512]{1,0:T(8,128)(2,1)} %get-tuple-element.11.refs_1_, ...), custom_call_target="tpu_custom_call" | custom-call | tf_op jit(solution)/shard_map/finish/pallas_call | solution.py:675

commit v6 on v5

--- a/solution.py
+++ b/solution.py
@@ -364,10 +364,11 @@
     def _():
         def step(i, s):
             s_low = s.astype(bf16)
+            kept = s - dot(s_low, loss_all[i % 16, i // 16], NN)
             sent[i] = s_low
             give_back(i, sent, state, b_send, b_recv)
             landed(got.at[i], s_recv.at[i])
-            return s - dot(s_low, loss_all[i % 16, i // 16], NN) + got[i].astype(f32)
+            return kept + got[i].astype(f32)
 
         lax.fori_loop(0, n_row, step, jnp.zeros((16, 128), f32), unroll=UNROLL)
         state[a, lane_rows, :] = sent[me]
@@ -405,10 +406,11 @@
         def step(k, s):
             i = n_row - 1 - k
             s_low = s.astype(bf16)
+            kept = s - dot(s_low, loss_turned[i], NN)
             sent2[i] = s_low
             give_back(i, sent2, grad, u_send, u_recv)
             landed(got2.at[i], t_recv.at[i])
-            return s - dot(s_low, loss_turned[i], NN) + got2[i].astype(f32)
+            return kept + got2[i].astype(f32)
 
         lax.fori_loop(0, n_row, step, jnp.zeros((16, 128), f32), unroll=UNROLL)
         grad[a, lane_rows, :] = sent2[me]
@@ -451,7 +453,12 @@
         unit = rs * x.astype(f32)
         dk_ref[:, p] = (rs * (d_k - unit * jnp.sum(unit * d_k, axis=1, keepdims=True))).astype(bf16)
 
-    theirs = dv_all.at[pl.ds(pl.multiple_of((1 - a) * 128, 128), 128), :]
+    their_tokens = pl.ds(pl.multiple_of((1 - a) * 128, 128), 128)
+    theirs = dv_all.at[their_tokens, :]
+    early = [
+        dot(act_all[a, d // 2, d % 2], dv_all[own_tokens, :], TN)
+        for d in ((z + 8) % n_z, (z + n_z - 7) % n_z)
+    ]
     landed(theirs, dv_sem.at[1])
 
     def w_term(d):
@@ -550,8 +557,11 @@
             def _():
                 pltpu.make_async_copy(in_terms.at[t, cc, f], dst, sem).start()
 
-    r_make(0)
-    r_step(0)
+    for way in range(2):
+        d = r_dest(0, way)
+        term = early[way] + dot(act_all[1 - a, d // 2, d % 2], dv_all[their_tokens, :], TN)
+        w_terms[d] = term.astype(bf16)
+        r_send(0, way)
     for k in range(4):
         sib_send(k)
     r_make(1)

time: 129 us -> 129 us (level)
  no operation moved by 1% of the time
where the time goes in v6:
time: 129 us; the launch traced here: 128 us
  Pallas kernels  127 us (98%)
    pallas_call x1, Pallas kernels, layer(): pl.pallas_call(layer_kernel, out_shape=(o, jax.ShapeDtypeStruct((128, 512...  125 us

profile of v6, /device:TPU:6, one launch (start us, length us, event | category | flops | bytes accessed | tf_op | source)
XLA Modules:
  0.0 127.7 jit_solution(3246787492310893081)
XLA Ops:
  0.6 125.1 %layer.1 = (bf16[128,256]{1,0:T(8,128)(2,1)}, bf16[128,512]{1,0:T(8,128)(2,1)}, bf16[128,256]{1,0:T(8,128)(2,1)}, bf16[128,256]{1,0:T(8,128)(2,1)}, f32[256,256]{1,0:T(8,128)}) custom-call(bf16[128,512]{1,0:T(8,128)(2,1)} %act_hbm.1, bf16[256,256]{1,0:T(8,128)(2,1)} %w_hbm.1, bf16[128,256]{1,0:T(8,128)(2,1)} %q_hbm.1, bf16[128,256]{1,0:T(8,128)(2,1)} %x_hbm.1, ...), custom_call_target="tpu_custom_call" | custom-call | tf_op jit(solution)/shard_map/layer/pallas_call | solution.py:645
  125.8 1.9 %finish.1 = (bf16[128,256]{1,0:T(8,128)(2,1)}, bf16[128,512]{1,0:T(8,128)(2,1)}, bf16[128,256]{1,0:T(8,128)(2,1)}, bf16[128,256]{1,0:T(8,128)(2,1)}, f32[256,256]{1,0:T(8,128)}) custom-call(bf16[128,256]{1,0:T(8,128)(2,1)} %get-tuple-element.10.refs_0_, bf16[128,512]{1,0:T(8,128)(2,1)} %get-tuple-element.11.refs_1_, ...), custom_call_target="tpu_custom_call" | custom-call | tf_op jit(solution)/shard_map/finish/pallas_call | solution.py:685
